TPU v7x, 32 devices: a whole 2x2x4 slice. The times are simulated.
32 devices in a mesh: groups: 2 (over y), mpo: 4 (over z), sector: 4 (over x, core).
Axes of the slice: x: 2, y: 2, z: 4, core: 2. Of those that a mesh axis runs over, the one named last changes fastest.
Arguments:
- psi: bfloat16 [16, 128, 16, 128], P(('groups', 'sector')), parts along dimension 0, may hold values from -6 to 6
- left_env: bfloat16 [4, 128, 128, 128], P('mpo', ('groups', 'sector')), parts along dimension 1, may hold values from -0.5 to 0.5
- mpo: bfloat16 [8, 4, 16, 16], P(('groups', 'mpo')), parts along dimension 0, may hold values from -0.75 to 0.75
- right_env: bfloat16 [4, 128, 128, 128], P('mpo', ('groups', 'sector')), parts along dimension 1, may hold values from -0.25 to 0.25
- left_local: int32 [16], P('groups'), parts along dimension 0, may hold values from 0 to 15
- right_owner: int32 [16], P('groups'), parts along dimension 0, may hold values from 0 to 3, as said below
- right_local: int32 [16], P('groups'), parts along dimension 0, may hold values from 0 to 15
Outputs:
- h_psi: bfloat16 [16, 262144], P(('groups', 'sector'), 'mpo'), parts along dimension 0
There are 2 independent parts, one for each index of `groups`. A program takes and returns all parts, laid end to end along the dimension named above; each array names one. Nothing has to cross between parts.
Inputs may be any that keep to these rules, and one draw needn't show every extreme that they name: `right_owner`: two indices of sector have all their blocks' right sectors owned by one common index, which owns exactly 4 blocks' right sectors; no block of any other index goes to that owner, and no index owns more than 4.
All inputs are finite; a program needn't handle non-finite values.
Results may differ from a plain program's by a relative error of at most 0.0058.
Values may be sent and summed in bfloat16 or wider, within the bound.
A program may use at most 128 MiB of HBM per device.

v0:
```python
import jax
import jax.numpy as jnp
from jax import lax
from jax.sharding import PartitionSpec as P


def apply_block(wrow, blocks, renv, count):

    def one_slot(pair):
        block, env = pair
        mixed = jnp.einsum("vqp,lpr->lqvr", wrow, block, preferred_element_type=jnp.float32).astype(
            jnp.bfloat16
        )
        return jnp.einsum("lqvr,vtr->lqt", mixed, env, preferred_element_type=jnp.float32)

    terms = lax.map(one_slot, (blocks, renv))
    return jnp.moveaxis(terms, 0, 1).reshape(count, blocks.shape[0], -1)


def partial_sums(wrow, blocks, renv, local_rows):
    return lax.psum_scatter(
        apply_block(wrow, blocks, renv, local_rows * lax.axis_size("mpo")),
        "mpo",
        scatter_dimension=0,
        tiled=True,
    )


def finish(mpo, blocks, renv, local_rows):
    return partial_sums(mpo[0], blocks, renv, local_rows)


def collect_env(pieces):
    return lax.all_gather(pieces[:, None], "mpo", axis=1, tiled=True)


def body(psi, left_env, mpo, right_env, left_local, right_owner, right_local):
    blk_dev, rows, phys, width = psi.shape
    nsec = lax.axis_size("sector")
    nmpo = lax.axis_size("mpo")
    local_rows = rows // nmpo
    me = lax.axis_index("sector")
    first = me * blk_dev
    mine_left = lax.dynamic_slice_in_dim(left_local, first, blk_dev)
    mine_owner = lax.dynamic_slice_in_dim(right_owner, first, blk_dev)
    lenv = jnp.take(left_env[0], mine_left, axis=0)
    flat = psi.reshape(blk_dev, rows, phys * width)
    moved = jnp.einsum("kml,klf->kmf", lenv, flat, preferred_element_type=jnp.float32).astype(
        jnp.bfloat16
    )
    moved = moved.reshape(blk_dev, rows, phys, width)
    targets = jnp.arange(nsec, dtype=jnp.int32)
    landed = mine_owner[None, :] == targets[:, None]
    here = right_owner == me
    wanted = jnp.take(right_env[0], right_local, axis=0)
    outgoing = jnp.where(here[:, None, None], wanted, jnp.zeros((), jnp.bfloat16)).reshape(
        nsec, blk_dev, rows, rows
    )
    arrived = lax.all_to_all(outgoing, "sector", split_axis=0, concat_axis=0, tiled=True)
    own_env = jnp.sum(
        jnp.where(landed[:, :, None, None], arrived, jnp.zeros((), jnp.bfloat16)), axis=0
    )
    renv = collect_env(own_env)
    result = finish(mpo, moved, renv, local_rows).astype(jnp.bfloat16)
    return jnp.moveaxis(result, 0, 1).reshape(blk_dev, local_rows * phys * width)


def solution(mesh):
    placed = (
        P(("groups", "sector"), None, None, None),
        P("mpo", ("groups", "sector"), None, None),
        P(("groups", "mpo"), None, None, None),
        P("mpo", ("groups", "sector"), None, None),
        P("groups"),
        P("groups"),
        P("groups"),
    )
    return jax.shard_map(
        body, mesh=mesh, in_specs=placed, out_specs=P(("groups", "sector"), "mpo"), check_vma=False
    )
```

profile of v0, /device:TPU:0, one launch (start us, length us, event | category | flops | bytes accessed | tf_op | source)
XLA Modules:
  0.0 115.4 jit_solution(4334914721744203806)
XLA Ops:
  0.0 0.0 copy-start
  0.0 0.8 compare_select_fusion
  0.8 0.7 compare_and_fusion
  1.4 0.7 broadcast_compare_fusion
  2.1 0.1 broadcast_in_dim.69
  2.2 0.1 broadcast_in_dim.71
  2.3 0.0 copy-done
  2.3 0.6 gather_fusion.1
  2.9 0.8 select_select_fusion
  3.7 4.2 %all-to-all-start = ((bf16[4,2,128,128]{3,2,1,0:T(8,128)(2,1)}), bf16[4,2,128,128]{3,2,1,0:T(8,128)(2,1)S(1)}, u32[]{:S(2)}, u32[]{:S(2)}) async-start(bf16[4,2,128,128]{3,2,1,0:T(8,128)(2,1)} %select_select_fusion), calls=%async_computation | async-start | bytes 524288 | tf_op jit(solution)/shard_map/all_to_all | solution.py:59
  7.9 0.7 dynamic_slice.15
  8.6 0.7 compare_and_fusion.1
  9.4 0.0 copy-done.1
  9.4 0.5 reshape.47
  9.9 1.6 %gather_fusion = bf16[2,128,128]{2,1,0:T(8,128)(2,1)S(1)} fusion(bf16[16,128,128]{2,1,0:T(8,128)(2,1)} %bitcast.57, s32[1024]{0:T(1024)S(1)} %pad_clamp_fusion.1), kind=kCustom, calls=%fused_computation | custom fusion | bytes 131080 | tf_op jit(solution)/shard_map/jit(_take)/gather | solution.py:46
  11.5 0.0 copy-start.3
  11.5 0.0 copy-start.2
  11.5 0.5 convolution_convert_fusion
  12.0 0.2 copy.19
  12.3 0.6 dynamic-slice
  13.5 0.4 all-to-all-done
  13.9 0.1 select_reduce_fusion
  14.1 14.6 %all-gather = bf16[2,512,128]{2,1,0:T(8,128)(2,1)S(1)} all-gather(bf16[2,128,128]{2,1,0:T(8,128)(2,1)S(1)} %select_reduce_fusion), channel_id=2, replica_groups=mesh['groups'=2,'mpo'=4,'sector'=4] {'mpo'}, dimensions={1}, use_global_device_ids=true | all-gather | bytes 327680 | tf_op jit(solution)/shard_map/all_gather | solution.py:34
  28.7 0.0 copy-done.2
  28.7 8.4 %while.10 = (s32[]{:T(128)}, f32[2,128,16,128]{1,3,2,0:T(8,128)}, bf16[2,128,16,128]{3,2,1,0:T(8,128)(2,1)S(1)}, bf16[4,16,16]{2,1,0:T(8,128)(2,1)S(1)}, bf16[2,4,128,128]{3,2,1,0:T(8,128)(2,1)S(1)}, /*index=5*/s32[]{:T(128)}) while((s32[]{:T(128)}, f32[2,128,16,128]{1,3,2,0:T(8,128)}, bf16[2,128,16,128]{3,2,1,0:T(8,128)(2,1)S(1)}, ...), condition=%wide.region_2.3_spmd, body=%wide.region_1.2_spmd.sunk | while | flops 303038464 | bytes 5915721 | solution.py:16
  28.7 0.7 convert_bitcast_fusion.2
  29.4 3.5 %fusion.29 = f32[2,128,16,128]{1,3,2,0:T(8,128)} fusion(f32[2,128,16,128]{1,3,2,0:T(8,128)} %get-tuple-element.83, s32[]{:T(128)} %get-tuple-element.82, bf16[128,16,4,128]{3,1,2,0:T(8,128)(2,1)S(1)} %convert_bitcast_fusion.2, bf16[2,4,128,128]{3,2,1,0:T(8,128)(2,1)S(1)} %get-tuple-element.92), kind=kOutput, calls=%fused_computation.6.clone.1 | convolution fusion | flops 268435456 | bytes 3277824 | tf_op jit(solution)/shard_map/while/body/eval_jaxpr/lqvr,vtr->lqt/dot_general | solution.py:14
  32.9 0.7 convert_bitcast_fusion.2
  33.6 3.5 %fusion.29 = f32[2,128,16,128]{1,3,2,0:T(8,128)} fusion(f32[2,128,16,128]{1,3,2,0:T(8,128)} %get-tuple-element.83, s32[]{:T(128)} %get-tuple-element.82, bf16[128,16,4,128]{3,1,2,0:T(8,128)(2,1)S(1)} %convert_bitcast_fusion.2, bf16[2,4,128,128]{3,2,1,0:T(8,128)(2,1)S(1)} %get-tuple-element.92), kind=kOutput, calls=%fused_computation.6.clone.1 | convolution fusion | flops 268435456 | bytes 3277824 | tf_op jit(solution)/shard_map/while/body/eval_jaxpr/lqvr,vtr->lqt/dot_general | solution.py:14
  37.1 2.9 %copy.14 = f32[128,2,2048]{2,1,0:T(2,128)S(1)} copy(f32[128,2,2048]{0,2,1:T(8,128)} %bitcast.16) | data formatting | bytes 4194304 | tf_op jit(solution)/shard_map/reshape | solution.py:17
  40.0 73.5 %all-reduce.2 = bf16[128,2,2048]{2,1,0:T(2,128)(2,1)} all-reduce(f32[128,2,2048]{2,1,0:T(2,128)S(1)} %copy.14), channel_id=3, replica_groups=mesh['groups'=2,'mpo'=4,'sector'=4] {'mpo'}, use_global_device_ids=true, to_apply=%region_3.4.clone | all-reduce | flops 524288 | bytes 3145728
  113.5 1.8 %dynamic-slice_convert_fusion = bf16[32,2,2048]{2,1,0:T(2,128)(2,1)} fusion(bf16[128,2,2048]{2,1,0:T(2,128)(2,1)} %all-reduce.2, u32[]{:T(128)S(6)} %multiply.1), kind=kLoop, calls=%fused_computation.15 | loop fusion | bytes 524292 | tf_op jit(solution)/shard_map/convert_element_type | solution.py:64
  (6 shorter events, 0.0 us)
Async XLA Ops:
  0.0 2.3 %copy-start = (bf16[1,16,128,128]{3,2,1,0:T(8,128)(2,1)S(1)}, bf16[1,16,128,128]{3,2,1,0:T(8,128)(2,1)}, u32[]{:S(2)}) copy-start(bf16[1,16,128,128]{3,2,1,0:T(8,128)(2,1)} %param.12) | copy-start | bytes 1572868
  0.0 9.4 %copy-start.1 = (bf16[2,128,16,128]{3,2,1,0:T(8,128)(2,1)S(1)}, bf16[2,128,16,128]{3,2,1,0:T(8,128)(2,1)}, u32[]{:S(2)}) copy-start(bf16[2,128,16,128]{3,2,1,0:T(8,128)(2,1)} %param.9) | copy-start | bytes 3145732
  3.7 10.2 %all-to-all-start = ((bf16[4,2,128,128]{3,2,1,0:T(8,128)(2,1)}), bf16[4,2,128,128]{3,2,1,0:T(8,128)(2,1)S(1)}, u32[]{:S(2)}, u32[]{:S(2)}) async-start(bf16[4,2,128,128]{3,2,1,0:T(8,128)(2,1)} %select_select_fusion), calls=%async_computation | async-start | bytes 524288 | tf_op jit(solution)/shard_map/all_to_all | solution.py:59
  11.5 0.7 copy-start.3
  11.5 17.2 %copy-start.2 = (bf16[1,4,16,16]{3,2,1,0:T(8,128)(2,1)S(1)}, bf16[1,4,16,16]{3,2,1,0:T(8,128)(2,1)}, u32[]{:S(2)}) copy-start(bf16[1,4,16,16]{3,2,1,0:T(8,128)(2,1)} %param.11) | copy-start | bytes 6148
where the time goes:
time: 116 us; the launch traced here: 115 us
  blocking collectives  88.2 us (76%)
  local copies, waits for them, and re-layouts  9.26 us (8%)
  matrix products  8.81 us (8%)
  starting transfers between devices  4.21 us (4%)
  other arithmetic  3.77 us (3%)
    unnamed x1, blocking collectives  73.5 us
    all_gather x1, blocking collectives, collect_env(): return lax.all_gather(pieces[:, None], 'mpo', axis=1, tiled=True)  14.6 us
    dot_general x2, matrix products, one_slot(): jnp.einsum('lqvr,vtr->lqt', mixed, env, preferred_element_type=jnp.float32)  6.99 us
    all_to_all x1, starting transfers between devices, body(): lax.all_to_all(outgoing, 'sector', split_axis=0, concat_axis=0, tiled=True)  4.21 us
    reshape x1, local copies, waits for them, and re-layouts, apply_block(): return jnp.moveaxis(terms, 0, 1).reshape(count, blocks.shape[0], -1)  2.94 us
  transfers between devices with their start and end apart: 1, of which 1 were waited for; matrix products, arithmetic and copies ran while one was open for 4% of the time, Pallas kernels for 0%

commit v1 on v0

v1 whole, which is shorter than its diff:
```python
import jax
import jax.numpy as jnp
from jax import lax
from jax.sharding import PartitionSpec as P

F32 = jnp.float32
BF16 = jnp.bfloat16


def body(psi, left_env, mpo, right_env, left_local, right_owner, right_local):
    blk_dev, rows, phys, width = psi.shape
    nsec = lax.axis_size("sector")
    nmpo = lax.axis_size("mpo")
    local_rows = rows // nmpo
    me = lax.axis_index("sector")
    first = me * blk_dev
    slots = jnp.where(right_owner == me, right_local, 0)
    wanted = [lax.dynamic_index_in_dim(right_env[0], slots[i], 0) for i in range(nsec * blk_dev)]
    outgoing = jnp.concatenate(wanted).reshape(nsec, blk_dev, rows, width)
    arrived = lax.all_to_all(outgoing, "sector", split_axis=0, concat_axis=0, tiled=True)

    own_left, own_env = [], []
    for i in range(blk_dev):
        own_left.append(
            lax.dynamic_index_in_dim(left_env[0], left_local[first + i], 0).reshape(nmpo, local_rows, rows)
        )
        own_env.append(lax.dynamic_index_in_dim(arrived[:, i], right_owner[first + i], 0))
    env_rows = blk_dev * rows
    own_env = jnp.concatenate(own_env).reshape(1, env_rows, width)
    left_rows = blk_dev * local_rows
    own_mpo = mpo[0].reshape(1, -1, width)
    packed = jnp.concatenate(
        own_left
        + [
            jnp.broadcast_to(own_env, (nmpo, env_rows, width)),
            jnp.broadcast_to(own_mpo, (nmpo,) + own_mpo.shape[1:]),
        ],
        axis=1,
    )
    got = lax.all_to_all(packed, "mpo", split_axis=0, concat_axis=0, tiled=True)
    lenv = got[:, :left_rows].reshape(nmpo, blk_dev, local_rows, rows)
    renv = got[:, left_rows : left_rows + env_rows].reshape(nmpo, blk_dev, rows, width)
    tensor = got[:, left_rows + env_rows :].reshape((nmpo,) + mpo.shape[1:])

    moved = jnp.einsum("wkml,klpr->kmwpr", lenv, psi, preferred_element_type=F32).astype(BF16)
    mixed = jnp.einsum("wvqp,kmwpr->kmqvr", tensor, moved, preferred_element_type=F32).astype(BF16)
    result = jnp.einsum("kmqvr,vktr->kmqt", mixed, renv, preferred_element_type=F32).astype(BF16)
    return result.reshape(blk_dev, local_rows * phys * width)


def solution(mesh):
    placed = (
        P(("groups", "sector"), None, None, None),
        P("mpo", ("groups", "sector"), None, None),
        P(("groups", "mpo"), None, None, None),
        P("mpo", ("groups", "sector"), None, None),
        P("groups"),
        P("groups"),
        P("groups"),
    )
    return jax.shard_map(
        body, mesh=mesh, in_specs=placed, out_specs=P(("groups", "sector"), "mpo"), check_vma=False
    )
```

time: 116 us -> 60.8 us (0.52)
  blocking collectives: 88.2 us -> 16.4 us
  between operations: 0.73 us -> 22.6 us
  matrix products: 8.81 us -> 1.25 us
  local copies, waits for them, and re-layouts: 9.26 us -> 14.4 us
  other arithmetic: 3.77 us -> 0.8 us
    unnamed x1 -> x0, blocking collectives: 73.5 us -> none
    all_to_all x0 -> x1, blocking collectives: none -> 16.4 us  [body(): got = lax.all_to_all(packed, 'mpo', split_axis=0, concat_axis=0, tiled=True)]
    all_gather x1 -> x0, blocking collectives: 14.6 us -> none  [collect_env(): return lax.all_gather(pieces[:, None], 'mpo', axis=1, tiled=True)]
    unnamed x10 -> x16, local copies, waits for them, and re-layouts: 0.89 us -> 10.6 us
    dot_general x5 -> x2, matrix products: 8.81 us -> 1.25 us  [the longest x1 0.82 us: body(): jnp.einsum('kmqvr,vktr->kmqt', mixed, renv, preferred_element_type=F32)]
    reshape x2 -> x1, local copies, waits for them, and re-layouts: 3.44 us -> 0.1 us  [body(): tensor = got[:, left_rows + env_rows:].reshape((nmpo,) + mpo.shape[1:])]
    gather x2 -> x0, local copies, waits for them, and re-layouts: 2.21 us -> none  [the longest x1 1.61 us: body(): lenv = jnp.take(left_env[0], mine_left, axis=0)]
    convert_element_type x1 -> x0, local copies, waits for them, and re-layouts: 1.83 us -> none  [body(): result = finish(mpo, moved, renv, local_rows).astype(jnp.bfloat16)]
  transfers between devices with their start and end apart: 1 -> 1, of which waited for: 1 -> 0; matrix products, arithmetic and copies ran while one was open for 4% -> 3% of each run, Pallas kernels for 0% -> 0%
where the time goes in v1:
time: 60.8 us; the launch traced here: 59.7 us
  between operations  22.6 us (37%)
  blocking collectives  16.4 us (27%)
  local copies, waits for them, and re-layouts  14.4 us (24%)
  starting transfers between devices  4.21 us (7%)
  matrix products  1.25 us (2%)
  other arithmetic  0.8 us (1%)
    all_to_all x1, blocking collectives, body(): got = lax.all_to_all(packed, 'mpo', split_axis=0, concat_axis=0, tiled=True)  16.4 us
    unnamed x16, local copies, waits for them, and re-layouts  10.6 us
    all_to_all x1, starting transfers between devices, body(): lax.all_to_all(outgoing, 'sector', split_axis=0, concat_axis=0, tiled=True)  4.21 us
    concatenate x1, local copies, waits for them, and re-layouts, body(): outgoing = jnp.concatenate(wanted).reshape(nsec, blk_dev, rows, width)  1.37 us
  transfers between devices with their start and end apart: 1, of which 0 were waited for; matrix products, arithmetic and copies ran while one was open for 3% of the time, Pallas kernels for 0%

profile of v1, /device:TPU:0, one launch (start us, length us, event | category | flops | bytes accessed | tf_op | source)
XLA Modules:
  0.0 59.7 jit_solution(13316732001329913401)
XLA Ops:
  0.0 0.0 copy-start
  0.0 0.0 copy-start.2
  0.0 0.0 copy-start.3
  0.0 0.0 copy-start.1
  0.0 0.8 %compare_select_fusion = s32[8]{0:T(128)S(1)} fusion(s32[8]{0:T(128)} %param.13, s32[8]{0:T(128)} %param.12, s32[]{:T(128)S(6)} %axis_index.12), kind=kLoop, calls=%fused_computation.28 | loop fusion | flops 16 | bytes 100 | tf_op jit(solution)/shard_map/jit(_where)/select_n | solution.py:17
  0.8 0.7 %fusion.16 = (s32[1]{0:T(128)}, s32[1]{0:T(128)}, s32[1]{0:T(128)}, s32[1]{0:T(128)}, s32[1]{0:T(128)}, /*index=5*/s32[1]{0:T(128)}, s32[1]{0:T(128)}, s32[1]{0:T(128)}) fusion(s32[8]{0:T(128)S(1)} %compare_select_fusion), kind=kLoop, calls=%fused_computation.32 | loop fusion | bytes 64 | tf_op jit(solution)/shard_map/slice | solution.py:18
  16.4 1.4 %bitcast_dynamic-update-slice_fusion.7 = bf16[8,128,128]{2,1,0:T(8,128)(2,1)} fusion(bf16[1,16,128,128]{3,2,1,0:T(8,128)(2,1)} %param.10, s32[]{:T(128)S(6)} %select_n.55), kind=kLoop, calls=%fused_computation.23 | loop fusion | bytes 65540
  17.7 1.4 %bitcast_dynamic-update-slice_fusion.6 = bf16[8,128,128]{2,1,0:T(8,128)(2,1)} fusion(bf16[8,128,128]{2,1,0:T(8,128)(2,1)} %bitcast_dynamic-update-slice_fusion.7, bf16[1,16,128,128]{3,2,1,0:T(8,128)(2,1)} %param.10, s32[]{:T(128)S(6)} %select_n.56), kind=kLoop, calls=%fused_computation.22 | loop fusion | bytes 65540
  19.1 1.4 %bitcast_dynamic-update-slice_fusion.5 = bf16[8,128,128]{2,1,0:T(8,128)(2,1)} fusion(bf16[8,128,128]{2,1,0:T(8,128)(2,1)} %bitcast_dynamic-update-slice_fusion.6, bf16[1,16,128,128]{3,2,1,0:T(8,128)(2,1)} %param.10, s32[]{:T(128)S(6)} %select_n.57), kind=kLoop, calls=%fused_computation.21 | loop fusion | bytes 65540
  20.5 1.4 %bitcast_dynamic-update-slice_fusion.4 = bf16[8,128,128]{2,1,0:T(8,128)(2,1)} fusion(bf16[8,128,128]{2,1,0:T(8,128)(2,1)} %bitcast_dynamic-update-slice_fusion.5, bf16[1,16,128,128]{3,2,1,0:T(8,128)(2,1)} %param.10, s32[]{:T(128)S(6)} %select_n.58), kind=kLoop, calls=%fused_computation.20 | loop fusion | bytes 65540
  21.9 1.4 %bitcast_dynamic-update-slice_fusion.3 = bf16[8,128,128]{2,1,0:T(8,128)(2,1)} fusion(bf16[8,128,128]{2,1,0:T(8,128)(2,1)} %bitcast_dynamic-update-slice_fusion.4, bf16[1,16,128,128]{3,2,1,0:T(8,128)(2,1)} %param.10, s32[]{:T(128)S(6)} %select_n.59), kind=kLoop, calls=%fused_computation.19 | loop fusion | bytes 65540
  23.2 1.4 %bitcast_dynamic-update-slice_fusion.2 = bf16[8,128,128]{2,1,0:T(8,128)(2,1)} fusion(bf16[8,128,128]{2,1,0:T(8,128)(2,1)} %bitcast_dynamic-update-slice_fusion.3, bf16[1,16,128,128]{3,2,1,0:T(8,128)(2,1)} %param.10, s32[]{:T(128)S(6)} %select_n.60), kind=kLoop, calls=%fused_computation.18 | loop fusion | bytes 65540
  24.6 1.4 %bitcast_dynamic-update-slice_fusion.1 = bf16[8,128,128]{2,1,0:T(8,128)(2,1)} fusion(bf16[8,128,128]{2,1,0:T(8,128)(2,1)} %bitcast_dynamic-update-slice_fusion.2, bf16[1,16,128,128]{3,2,1,0:T(8,128)(2,1)} %param.10, s32[]{:T(128)S(6)} %select_n.61), kind=kLoop, calls=%fused_computation.17 | loop fusion | bytes 65540
  26.0 1.4 %bitcast_dynamic-update-slice_fusion = bf16[8,128,128]{2,1,0:T(8,128)(2,1)} fusion(bf16[8,128,128]{2,1,0:T(8,128)(2,1)} %bitcast_dynamic-update-slice_fusion.1, bf16[1,16,128,128]{3,2,1,0:T(8,128)(2,1)} %param.10, s32[]{:T(128)S(6)} %select_n.62), kind=kLoop, calls=%fused_computation.16 | loop fusion | bytes 65540 | tf_op jit(solution)/shard_map/concatenate | solution.py:19
  27.4 4.2 %all-to-all-start = ((bf16[4,2,128,128]{3,2,1,0:T(8,128)(2,1)}), bf16[4,2,128,128]{3,2,1,0:T(8,128)(2,1)S(1)}, u32[]{:S(2)}, u32[]{:S(2)}) async-start(bf16[4,2,128,128]{3,2,1,0:T(8,128)(2,1)} %bitcast.20), calls=%async_computation | async-start | bytes 524288 | tf_op jit(solution)/shard_map/all_to_all | solution.py:20
  31.6 0.0 copy-done.2
  31.6 0.0 copy-done.3
  31.6 0.7 %fusion.14 = (s32[1]{0:T(128)}, s32[1]{0:T(128)}, s32[1]{0:T(128)}, s32[1]{0:T(128)}) fusion(s32[8]{0:T(128)S(1)} %copy-done.3, s32[]{:T(128)S(6)} %select_n.50, s32[]{:T(128)S(6)} %select_n.52, s32[8]{0:T(128)S(1)} %copy-done.2), kind=kLoop, calls=%fused_computation.30 | loop fusion | bytes 40 | tf_op jit(solution)/shard_map/dynamic_slice | solution.py:25
  37.3 0.0 copy-done.1
  37.3 0.1 broadcast_in_dim.21
  39.9 0.8 %constant_dynamic-slice_fusion.1 = (bf16[1,1,128,128]{3,2,1,0:T(8,128)(2,1)S(1)}, bf16[1,1,128,128]{3,2,1,0:T(8,128)(2,1)S(1)}) fusion(bf16[1,16,128,128]{3,2,1,0:T(8,128)(2,1)} %param.8, s32[]{:T(128)S(6)} %select_n.51, s32[]{:T(128)S(6)} %select_n.53), kind=kLoop, calls=%fused_computation.27 | loop fusion | bytes 131080 | tf_op jit(solution)/shard_map/jit(dynamic_index_in_dim)/dynamic_slice | solution.py:25
  40.7 0.0 all-to-all-done
  40.9 16.4 %all_to_all.10 = bf16[4,328,128]{2,1,0:T(8,128)(2,1)S(1)} all-to-all(bf16[4,328,128]{2,1,0:T(8,128)(2,1)S(1)} %pad_maximum_fusion), channel_id=1, replica_groups=mesh['groups'=2,'mpo'=4,'sector'=4] {'mpo'}, dimensions={0} | all-to-all | bytes 671744 | tf_op jit(solution)/shard_map/all_to_all | solution.py:40
  57.3 0.1 reshape.48
  57.4 0.0 copy-done
  57.4 0.4 fusion.7
  57.9 0.8 %fusion.3 = bf16[2,32,16,128]{3,2,1,0:T(8,128)(2,1)S(1)} fusion(bf16[4,2,128,128,1]{3,2,1,0,4:T(8,128)(2,1)S(1)} %bitcast.84, bf16[4,4,16,16,1,1]{3,2,1,0,4,5:T(8,128)(2,1)S(1)} %reshape.48, bf16[2,4,32,16,128]{4,2,3,1,0:T(8,128)(2,1)S(1)} %fusion.7), kind=kOutput, calls=%fused_computation.5 | convolution fusion | flops 201981952 | bytes 1581056 | tf_op jit(solution)/shard_map/kmqvr,vktr->kmqt/dot_general | solution.py:47
  58.7 1.0 %copy.39 = bf16[1,2,512,128]{3,1,2,0:T(2,128)(2,1)} copy(bf16[1,2,512,128]{3,2,1,0:T(8,128)(2,1)S(1)} %bitcast.85) | data formatting | bytes 524288
  (10 shorter events, 0.1 us)
Async XLA Ops:
  0.0 57.4 %copy-start = (bf16[2,128,16,128]{3,2,1,0:T(8,128)(2,1)S(1)}, bf16[2,128,16,128]{3,2,1,0:T(8,128)(2,1)}, u32[]{:S(2)}) copy-start(bf16[2,128,16,128]{3,2,1,0:T(8,128)(2,1)} %param.7) | copy-start | bytes 3145732
  0.0 31.6 %copy-start.2 = (s32[8]{0:T(128)S(1)}, s32[8]{0:T(128)}, u32[]{:S(2)}) copy-start(s32[8]{0:T(128)} %param.12) | copy-start | bytes 100
  0.0 31.6 %copy-start.3 = (s32[8]{0:T(128)S(1)}, s32[8]{0:T(128)}, u32[]{:S(2)}) copy-start(s32[8]{0:T(128)} %param.11) | copy-start | bytes 100
  0.0 37.3 %copy-start.1 = (bf16[1,4,16,16]{3,2,1,0:T(8,128)(2,1)S(1)}, bf16[1,4,16,16]{3,2,1,0:T(8,128)(2,1)}, u32[]{:S(2)}) copy-start(bf16[1,4,16,16]{3,2,1,0:T(8,128)(2,1)} %param.9) | copy-start | bytes 6148
  27.4 13.3 %all-to-all-start = ((bf16[4,2,128,128]{3,2,1,0:T(8,128)(2,1)}), bf16[4,2,128,128]{3,2,1,0:T(8,128)(2,1)S(1)}, u32[]{:S(2)}, u32[]{:S(2)}) async-start(bf16[4,2,128,128]{3,2,1,0:T(8,128)(2,1)} %bitcast.20), calls=%async_computation | async-start | bytes 524288 | tf_op jit(solution)/shard_map/all_to_all | solution.py:20

commit v2 on v1

--- a/solution.py
+++ b/solution.py
@@ -1,16 +1,200 @@
+import functools
+
 import jax
 import jax.numpy as jnp
 from jax import lax
+from jax.experimental import pallas as pl
+from jax.experimental.pallas import tpu as pltpu
 from jax.sharding import PartitionSpec as P
 
 F32 = jnp.float32
 BF16 = jnp.bfloat16
-
-
-def body(psi, left_env, mpo, right_env, left_local, right_owner, right_local):
-    blk_dev, rows, phys, width = psi.shape
-    nsec = lax.axis_size("sector")
-    nmpo = lax.axis_size("mpo")
+MESH = pl.DeviceIdType.MESH
+
+
+def exchange(
+    nsec,
+    nmpo,
+    left_local,
+    right_owner,
+    right_local,
+    left_env,
+    right_env,
+    mpo,
+    lenv,
+    renv,
+    tensor,
+    to_sector,
+    to_mpo,
+    sector_send,
+    sector_recv,
+    left_send,
+    left_recv,
+    tensor_send,
+    tensor_recv,
+    up_send,
+    down_send,
+    line_recv,
+    *from_sector,
+):
+    blk_dev, local_rows = lenv.shape[1], lenv.shape[2]
+    me = lax.axis_index("sector")
+    z = lax.axis_index("mpo")
+    barrier = pltpu.get_barrier_semaphore()
+    for d in range(1, nsec):
+        pl.semaphore_signal(barrier, inc=1, device_id={"sector": lax.rem(me + d, nsec)}, device_id_type=MESH)
+    for d in range(1, nmpo):
+        pl.semaphore_signal(barrier, inc=1, device_id={"mpo": lax.rem(z + d, nmpo)}, device_id_type=MESH)
+
+    for k in range(blk_dev):
+        for t in range(nsec):
+            to_sector[k, t] = right_env[right_local[t * blk_dev + k]]
+    for k in range(blk_dev):
+        picked = left_env[left_local[me * blk_dev + k]]
+        for j in range(nmpo):
+            to_mpo[j, k] = picked[j * local_rows : (j + 1) * local_rows]
+
+    pl.semaphore_wait(barrier, nsec + nmpo - 2)
+
+    def sector_copy(k, d):
+        peer = lax.rem(me + d, nsec)
+        return pltpu.make_async_remote_copy(
+            src_ref=to_sector.at[k, peer],
+            dst_ref=from_sector[k].at[me],
+            send_sem=sector_send.at[k, d],
+            recv_sem=sector_recv.at[k, d],
+            device_id={"sector": peer},
+            device_id_type=MESH,
+        )
+
+    def left_copy(d):
+        peer = lax.rem(z + d, nmpo)
+        return pltpu.make_async_remote_copy(
+            src_ref=to_mpo.at[peer],
+            dst_ref=lenv.at[z],
+            send_sem=left_send.at[d],
+            recv_sem=left_recv.at[d],
+            device_id={"mpo": peer},
+            device_id_type=MESH,
+        )
+
+    def tensor_copy(d):
+        return pltpu.make_async_remote_copy(
+            src_ref=mpo.at[0],
+            dst_ref=tensor.at[z],
+            send_sem=tensor_send.at[d],
+            recv_sem=tensor_recv.at[d],
+            device_id={"mpo": lax.rem(z + d, nmpo)},
+            device_id_type=MESH,
+        )
+
+    def line_copy(origin, k, up):
+        sems = up_send if up else down_send
+        return pltpu.make_async_remote_copy(
+            src_ref=renv.at[origin, k],
+            dst_ref=renv.at[origin, k],
+            send_sem=sems.at[origin, k],
+            recv_sem=line_recv.at[origin, k],
+            device_id={"mpo": z + 1 if up else z - 1},
+            device_id_type=MESH,
+        )
+
+    for k in range(blk_dev):
+        for d in range(1, nsec):
+            sector_copy(k, d).start()
+    for d in range(1, nmpo):
+        left_copy(d).start()
+        tensor_copy(d).start()
+    lenv[z] = to_mpo[z]
+    tensor[z] = mpo[0]
+
+    for k in range(blk_dev):
+        from_sector[k][me] = to_sector[k, me]
+        for d in range(1, nsec):
+            sector_copy(k, d).wait_recv()
+        renv[z, k] = from_sector[k][right_owner[me * blk_dev + k]]
+
+        @pl.when(z < nmpo - 1)
+        def _():
+            line_copy(z, k, True).start()
+
+        @pl.when(z > 0)
+        def _():
+            line_copy(z, k, False).start()
+
+    for d in range(1, nmpo):
+        for k in range(blk_dev):
+
+            @pl.when(z - d >= 0)
+            def _():
+                line_copy(z - d, k, True).wait_recv()
+
+                @pl.when(z < nmpo - 1)
+                def _():
+                    line_copy(z - d, k, True).start()
+
+            @pl.when(z + d < nmpo)
+            def _():
+                line_copy(z + d, k, False).wait_recv()
+
+                @pl.when(z > 0)
+                def _():
+                    line_copy(z + d, k, False).start()
+
+    for d in range(1, nmpo):
+        left_copy(d).wait()
+        tensor_copy(d).wait()
+    for k in range(blk_dev):
+        for d in range(1, nsec):
+            sector_copy(k, d).wait_send()
+        for d in range(nmpo):
+
+            @pl.when((z < nmpo - 1) & (z - d >= 0))
+            def _():
+                line_copy(z - d, k, True).wait_send()
+
+            @pl.when((z > 0) & (z + d < nmpo))
+            def _():
+                line_copy(z + d, k, False).wait_send()
+
+
+def gather(nsec, nmpo, mpo, left_env, right_env, left_local, right_owner, right_local, blk_dev):
+    rows, width = right_env.shape[2:]
+    local_rows = rows // nmpo
+    vmem = pl.BlockSpec(memory_space=pltpu.VMEM)
+    smem = pl.BlockSpec(memory_space=pltpu.SMEM)
+    dma = pltpu.SemaphoreType.DMA
+    return pl.pallas_call(
+        functools.partial(exchange, nsec, nmpo),
+        out_shape=(
+            jax.ShapeDtypeStruct((nmpo, blk_dev, local_rows, rows), BF16),
+            jax.ShapeDtypeStruct((nmpo, blk_dev, rows, width), BF16),
+            jax.ShapeDtypeStruct((nmpo,) + mpo.shape[1:], BF16),
+        ),
+        in_specs=[smem] * 3 + [vmem] * 3,
+        out_specs=(vmem,) * 3,
+        scratch_shapes=[
+            pltpu.VMEM((blk_dev, nsec, rows, width), BF16),
+            pltpu.VMEM((nmpo, blk_dev, local_rows, rows), BF16),
+            dma((blk_dev, nsec)),
+            dma((blk_dev, nsec)),
+            dma((nmpo,)),
+            dma((nmpo,)),
+            dma((nmpo,)),
+            dma((nmpo,)),
+            dma((nmpo, blk_dev)),
+            dma((nmpo, blk_dev)),
+            dma((nmpo, blk_dev)),
+        ]
+        + [pltpu.VMEM((nsec, rows, width), BF16)] * blk_dev,
+        compiler_params=pltpu.CompilerParams(
+            collective_id=0, has_side_effects=True, vmem_limit_bytes=24 * 2**20
+        ),
+    )(left_local, right_owner, right_local, left_env[0], right_env[0], mpo)
+
+
+def gather_plain(nsec, nmpo, mpo, left_env, right_env, left_local, right_owner, right_local, blk_dev):
+    rows, width = right_env.shape[2:]
     local_rows = rows // nmpo
     me = lax.axis_index("sector")
     first = me * blk_dev
@@ -42,6 +226,18 @@
     renv = got[:, left_rows : left_rows + env_rows].reshape(nmpo, blk_dev, rows, width)
     tensor = got[:, left_rows + env_rows :].reshape((nmpo,) + mpo.shape[1:])
 
+    return lenv, renv, tensor
+
+
+def body(psi, left_env, mpo, right_env, left_local, right_owner, right_local):
+    blk_dev, rows, phys, width = psi.shape
+    nsec = lax.axis_size("sector")
+    nmpo = lax.axis_size("mpo")
+    local_rows = rows // nmpo
+    collect = gather if local_rows % 16 == 0 else gather_plain
+    lenv, renv, tensor = collect(
+        nsec, nmpo, mpo, left_env, right_env, left_local, right_owner, right_local, blk_dev
+    )
     moved = jnp.einsum("wkml,klpr->kmwpr", lenv, psi, preferred_element_type=F32).astype(BF16)
     mixed = jnp.einsum("wvqp,kmwpr->kmqvr", tensor, moved, preferred_element_type=F32).astype(BF16)
     result = jnp.einsum("kmqvr,vktr->kmqt", mixed, renv, preferred_element_type=F32).astype(BF16)

time: 60.8 us -> 27.5 us (0.45); the launches traced: 59.7 us -> 27.2 us
  between operations: 22.6 us -> 0.03 us
  Pallas kernels: 0 us -> 18.9 us
  blocking collectives: 16.4 us -> 0 us
  local copies, waits for them, and re-layouts: 14.4 us -> 6.96 us
  starting transfers between devices: 4.21 us -> 0 us
  other arithmetic: 0.8 us -> 0 us
    pallas_call x0 -> x1, Pallas kernels: none -> 18.9 us  [gather(): pl.pallas_call(functools.partial(exchange, nsec, nmpo), out_shape=(jax.Sh...]
    all_to_all x1 -> x0, blocking collectives: 16.4 us -> none  [body(): got = lax.all_to_all(packed, 'mpo', split_axis=0, concat_axis=0, tiled=True)]
    all_to_all x1 -> x0, starting transfers between devices: 4.21 us -> none  [body(): lax.all_to_all(outgoing, 'sector', split_axis=0, concat_axis=0, tiled=True)]
    unnamed x16 -> x15, local copies, waits for them, and re-layouts: 10.6 us -> 6.96 us
    dynamic_slice x4 -> x0, local copies, waits for them, and re-layouts: 1.46 us -> none  [the longest x1 0.79 us: body(): lax.dynamic_index_in_dim(left_env[0], left_local[first + i], 0)]
    concatenate x1 -> x0, local copies, waits for them, and re-layouts: 1.37 us -> none  [body(): outgoing = jnp.concatenate(wanted).reshape(nsec, blk_dev, rows, width)]
    select_n x1 -> x0, other arithmetic: 0.76 us -> none  [body(): slots = jnp.where(right_owner == me, right_local, 0)]
    slice x5 -> x0, local copies, waits for them, and re-layouts: 0.7 us -> none  [the longest x1 0.66 us: body(): slots[i]]
  transfers between devices with their start and end apart: 1 -> 0, of which waited for: 0 -> 0; matrix products, arithmetic and copies ran while one was open for 3% -> 0% of each run, Pallas kernels for 0% -> 0%
where the time goes in v2:
time: 27.5 us; the launch traced here: 27.2 us
  Pallas kernels  18.9 us (69%)
  local copies, waits for them, and re-layouts  6.96 us (25%)
  matrix products  1.25 us (5%)
    pallas_call x1, Pallas kernels, gather(): pl.pallas_call(functools.partial(exchange, nsec, nmpo), out_shape=(jax.Sh...  18.9 us
    unnamed x15, local copies, waits for them, and re-layouts  6.96 us
    dot_general x1, matrix products, body(): jnp.einsum('kmqvr,vktr->kmqt', mixed, renv, preferred_element_type=F32)  0.82 us

profile of v2, /device:TPU:0, one launch (start us, length us, event | category | flops | bytes accessed | tf_op | source)
XLA Modules:
  0.0 27.2 jit_solution(1996351218989421024)
XLA Ops:
  0.0 0.0 copy-start
  0.0 1.2 %copy-done = bf16[2,128,16,128]{3,2,1,0:T(8,128)(2,1)S(1)} copy-done((bf16[2,128,16,128]{3,2,1,0:T(8,128)(2,1)S(1)}, bf16[2,128,16,128]{3,2,1,0:T(8,128)(2,1)}, u32[]{:S(2)}) %copy-start) | copy-done | bytes 1048600
  1.2 0.0 copy-start.1
  1.2 1.0 %copy-done.1 = bf16[1,16,128,128]{3,2,1,0:T(8,128)(2,1)S(1)} copy-done((bf16[1,16,128,128]{3,2,1,0:T(8,128)(2,1)S(1)}, bf16[1,16,128,128]{3,2,1,0:T(8,128)(2,1)}, u32[]{:S(2)}) %copy-start.1) | copy-done | bytes 524312
  2.3 0.0 copy-start.2
  2.3 1.0 %copy-done.2 = bf16[1,16,128,128]{3,2,1,0:T(8,128)(2,1)S(1)} copy-done((bf16[1,16,128,128]{3,2,1,0:T(8,128)(2,1)S(1)}, bf16[1,16,128,128]{3,2,1,0:T(8,128)(2,1)}, u32[]{:S(2)}) %copy-start.2) | copy-done | bytes 524312
  3.3 0.0 copy-start.3
  3.3 0.7 %copy-done.3 = bf16[1,4,16,16]{3,2,1,0:T(8,128)(2,1)S(1)} copy-done((bf16[1,4,16,16]{3,2,1,0:T(8,128)(2,1)S(1)}, bf16[1,4,16,16]{3,2,1,0:T(8,128)(2,1)}, u32[]{:S(2)}) %copy-start.3) | copy-done | bytes 2072
  4.0 0.0 copy-start.4
  4.0 0.7 %copy-done.4 = s32[8]{0:T(128)S(1)} copy-done((s32[8]{0:T(128)S(1)}, s32[8]{0:T(128)}, u32[]{:S(2)}) %copy-start.4) | copy-done | bytes 56
  4.7 0.0 copy-start.5
  4.7 0.7 %copy-done.5 = s32[8]{0:T(128)S(1)} copy-done((s32[8]{0:T(128)S(1)}, s32[8]{0:T(128)}, u32[]{:S(2)}) %copy-start.5) | copy-done | bytes 56
  5.3 0.0 copy-start.6
  5.3 0.7 %copy-done.6 = s32[8]{0:T(128)S(1)} copy-done((s32[8]{0:T(128)S(1)}, s32[8]{0:T(128)}, u32[]{:S(2)}) %copy-start.6) | copy-done | bytes 56
  6.0 18.9 %shard_map.73 = (bf16[4,2,32,128]{3,2,1,0:T(8,128)(2,1)S(1)}, bf16[4,2,128,128]{3,2,1,0:T(8,128)(2,1)S(1)}, bf16[4,4,16,16]{3,2,1,0:T(8,128)(2,1)S(1)}) custom-call(s32[8]{0:T(128)S(1)} %copy-done.4, s32[8]{0:T(128)S(1)} %copy-done.5, s32[8]{0:T(128)S(1)} %copy-done.6, bf16[16,128,128]{2,1,0:T(8,128)(2,1)S(1)} %bitcast.53, ...), custom_call_target="tpu_custom_call" | custom-call | tf_op jit(solution)/shard_map/pallas_call | solution.py:167
  24.9 0.4 %fusion.7 = bf16[2,4,32,16,128]{4,2,3,1,0:T(8,128)(2,1)S(1)} fusion(bf16[2,128,16,128,1]{3,2,1,0,4:T(8,128)(2,1)S(1)} %bitcast.52, bf16[4,2,32,128]{3,2,1,0:T(8,128)(2,1)S(1)} %get-tuple-element.8), kind=kOutput, calls=%fused_computation.8 | convolution fusion | flops 134217728 | bytes 2162688 | tf_op jit(solution)/shard_map/wkml,klpr->kmwpr/dot_general | solution.py:241
  25.4 0.8 %fusion.3 = bf16[2,32,16,128]{3,2,1,0:T(8,128)(2,1)S(1)} fusion(bf16[2,4,32,16,128]{4,2,3,1,0:T(8,128)(2,1)S(1)} %fusion.7, bf16[4,2,128,128]{3,2,1,0:T(8,128)(2,1)S(1)} %get-tuple-element.10, bf16[4,4,16,16]{3,2,1,0:T(8,128)(2,1)S(1)} %get-tuple-element.9), kind=kOutput, calls=%fused_computation.5 | convolution fusion | flops 201981952 | bytes 1581056 | tf_op jit(solution)/shard_map/kmqvr,vktr->kmqt/dot_general | solution.py:243
  26.2 1.0 %copy.39 = bf16[1,2,512,128]{3,1,2,0:T(2,128)(2,1)} copy(bf16[1,2,512,128]{3,2,1,0:T(8,128)(2,1)S(1)} %bitcast.55) | data formatting | bytes 524288
Async XLA Ops:
  0.0 1.2 %copy-start = (bf16[2,128,16,128]{3,2,1,0:T(8,128)(2,1)S(1)}, bf16[2,128,16,128]{3,2,1,0:T(8,128)(2,1)}, u32[]{:S(2)}) copy-start(bf16[2,128,16,128]{3,2,1,0:T(8,128)(2,1)} %param.7) | copy-start | bytes 3145732
  1.2 1.0 %copy-start.1 = (bf16[1,16,128,128]{3,2,1,0:T(8,128)(2,1)S(1)}, bf16[1,16,128,128]{3,2,1,0:T(8,128)(2,1)}, u32[]{:S(2)}) copy-start(bf16[1,16,128,128]{3,2,1,0:T(8,128)(2,1)} %param.8) | copy-start | bytes 1572868
  2.3 1.0 %copy-start.2 = (bf16[1,16,128,128]{3,2,1,0:T(8,128)(2,1)S(1)}, bf16[1,16,128,128]{3,2,1,0:T(8,128)(2,1)}, u32[]{:S(2)}) copy-start(bf16[1,16,128,128]{3,2,1,0:T(8,128)(2,1)} %param.10) | copy-start | bytes 1572868
  3.3 0.7 %copy-start.3 = (bf16[1,4,16,16]{3,2,1,0:T(8,128)(2,1)S(1)}, bf16[1,4,16,16]{3,2,1,0:T(8,128)(2,1)}, u32[]{:S(2)}) copy-start(bf16[1,4,16,16]{3,2,1,0:T(8,128)(2,1)} %mpo.1) | copy-start | bytes 6148
  4.0 0.7 %copy-start.4 = (s32[8]{0:T(128)S(1)}, s32[8]{0:T(128)}, u32[]{:S(2)}) copy-start(s32[8]{0:T(128)} %left_local.1) | copy-start | bytes 100
  4.7 0.7 %copy-start.5 = (s32[8]{0:T(128)S(1)}, s32[8]{0:T(128)}, u32[]{:S(2)}) copy-start(s32[8]{0:T(128)} %right_owner.1) | copy-start | bytes 100
  5.3 0.7 %copy-start.6 = (s32[8]{0:T(128)S(1)}, s32[8]{0:T(128)}, u32[]{:S(2)}) copy-start(s32[8]{0:T(128)} %right_local.1) | copy-start | bytes 100

commit v3 on v2

--- a/solution.py
+++ b/solution.py
@@ -15,15 +15,21 @@
 def exchange(
     nsec,
     nmpo,
+    left_local_hbm,
+    right_owner_hbm,
+    right_local_hbm,
+    left_env_hbm,
+    right_env_hbm,
+    mpo,
+    lenv,
+    renv,
+    tensor,
     left_local,
     right_owner,
     right_local,
     left_env,
     right_env,
-    mpo,
-    lenv,
-    renv,
-    tensor,
+    load_sem,
     to_sector,
     to_mpo,
     sector_send,
@@ -40,20 +46,32 @@
     blk_dev, local_rows = lenv.shape[1], lenv.shape[2]
     me = lax.axis_index("sector")
     z = lax.axis_index("mpo")
+    loads = [
+        pltpu.make_async_copy(src, dst, load_sem.at[i])
+        for i, (src, dst) in enumerate(
+            (
+                (right_local_hbm, right_local),
+                (right_env_hbm.at[0], right_env),
+                (left_local_hbm, left_local),
+                (left_env_hbm.at[0], left_env),
+                (right_owner_hbm, right_owner),
+                (mpo.at[0], tensor.at[z]),
+            )
+        )
+    ]
+    for load in loads:
+        load.start()
     barrier = pltpu.get_barrier_semaphore()
     for d in range(1, nsec):
         pl.semaphore_signal(barrier, inc=1, device_id={"sector": lax.rem(me + d, nsec)}, device_id_type=MESH)
     for d in range(1, nmpo):
         pl.semaphore_signal(barrier, inc=1, device_id={"mpo": lax.rem(z + d, nmpo)}, device_id_type=MESH)
 
+    loads[0].wait()
+    loads[1].wait()
     for k in range(blk_dev):
         for t in range(nsec):
             to_sector[k, t] = right_env[right_local[t * blk_dev + k]]
-    for k in range(blk_dev):
-        picked = left_env[left_local[me * blk_dev + k]]
-        for j in range(nmpo):
-            to_mpo[j, k] = picked[j * local_rows : (j + 1) * local_rows]
-
     pl.semaphore_wait(barrier, nsec + nmpo - 2)
 
     def sector_copy(k, d):
@@ -103,10 +121,18 @@
         for d in range(1, nsec):
             sector_copy(k, d).start()
     for d in range(1, nmpo):
+        tensor_copy(d).start()
+    loads[2].wait()
+    loads[3].wait()
+    for k in range(blk_dev):
+        picked = left_env[left_local[me * blk_dev + k]]
+        for j in range(nmpo):
+            to_mpo[j, k] = picked[j * local_rows : (j + 1) * local_rows]
+    for d in range(1, nmpo):
         left_copy(d).start()
-        tensor_copy(d).start()
     lenv[z] = to_mpo[z]
-    tensor[z] = mpo[0]
+    loads[4].wait()
+    loads[5].wait()
 
     for k in range(blk_dev):
         from_sector[k][me] = to_sector[k, me]
@@ -162,7 +188,7 @@
     rows, width = right_env.shape[2:]
     local_rows = rows // nmpo
     vmem = pl.BlockSpec(memory_space=pltpu.VMEM)
-    smem = pl.BlockSpec(memory_space=pltpu.SMEM)
+    hbm = pl.BlockSpec(memory_space=pl.ANY)
     dma = pltpu.SemaphoreType.DMA
     return pl.pallas_call(
         functools.partial(exchange, nsec, nmpo),
@@ -171,9 +197,15 @@
             jax.ShapeDtypeStruct((nmpo, blk_dev, rows, width), BF16),
             jax.ShapeDtypeStruct((nmpo,) + mpo.shape[1:], BF16),
         ),
-        in_specs=[smem] * 3 + [vmem] * 3,
+        in_specs=[hbm] * 6,
         out_specs=(vmem,) * 3,
         scratch_shapes=[
+            pltpu.SMEM(left_local.shape, left_local.dtype),
+            pltpu.SMEM(right_owner.shape, right_owner.dtype),
+            pltpu.SMEM(right_local.shape, right_local.dtype),
+            pltpu.VMEM(left_env.shape[1:], BF16),
+            pltpu.VMEM(right_env.shape[1:], BF16),
+            dma((6,)),
             pltpu.VMEM((blk_dev, nsec, rows, width), BF16),
             pltpu.VMEM((nmpo, blk_dev, local_rows, rows), BF16),
             dma((blk_dev, nsec)),
@@ -188,9 +220,9 @@
         ]
         + [pltpu.VMEM((nsec, rows, width), BF16)] * blk_dev,
         compiler_params=pltpu.CompilerParams(
-            collective_id=0, has_side_effects=True, vmem_limit_bytes=24 * 2**20
+            collective_id=0, has_side_effects=True, vmem_limit_bytes=40 * 2**20
         ),
-    )(left_local, right_owner, right_local, left_env[0], right_env[0], mpo)
+    )(left_local, right_owner, right_local, left_env, right_env, mpo)
 
 
 def gather_plain(nsec, nmpo, mpo, left_env, right_env, left_local, right_owner, right_local, blk_dev):

time: 27.5 us -> 27.1 us (0.985)
  Pallas kernels: 18.9 us -> 18.5 us
    pallas_call x1, Pallas kernels: 18.9 us -> 18.5 us  [gather(): pl.pallas_call(functools.partial(exchange, nsec, nmpo), out_shape=(jax.Sh...]
where the time goes in v3:
time: 27.1 us; the launch traced here: 26.8 us
  Pallas kernels  18.5 us (68%)
  local copies, waits for them, and re-layouts  6.96 us (26%)
  matrix products  1.25 us (5%)
    pallas_call x1, Pallas kernels, gather(): pl.pallas_call(functools.partial(exchange, nsec, nmpo), out_shape=(jax.Sh...  18.5 us
    unnamed x15, local copies, waits for them, and re-layouts  6.96 us
    dot_general x1, matrix products, body(): jnp.einsum('kmqvr,vktr->kmqt', mixed, renv, preferred_element_type=F32)  0.82 us

profile of v3, /device:TPU:0, one launch (start us, length us, event | category | flops | bytes accessed | tf_op | source)
XLA Modules:
  0.0 26.8 jit_solution(4601907294040804790)
XLA Ops:
  0.0 0.0 copy-start
  0.0 1.2 %copy-done = bf16[2,128,16,128]{3,2,1,0:T(8,128)(2,1)S(1)} copy-done((bf16[2,128,16,128]{3,2,1,0:T(8,128)(2,1)S(1)}, bf16[2,128,16,128]{3,2,1,0:T(8,128)(2,1)}, u32[]{:S(2)}) %copy-start) | copy-done | bytes 1048600
  1.2 0.0 copy-start.1
  1.2 1.0 %copy-done.1 = bf16[1,16,128,128]{3,2,1,0:T(8,128)(2,1)S(1)} copy-done((bf16[1,16,128,128]{3,2,1,0:T(8,128)(2,1)S(1)}, bf16[1,16,128,128]{3,2,1,0:T(8,128)(2,1)}, u32[]{:S(2)}) %copy-start.1) | copy-done | bytes 524312
  2.3 0.0 copy-start.2
  2.3 1.0 %copy-done.2 = bf16[1,16,128,128]{3,2,1,0:T(8,128)(2,1)S(1)} copy-done((bf16[1,16,128,128]{3,2,1,0:T(8,128)(2,1)S(1)}, bf16[1,16,128,128]{3,2,1,0:T(8,128)(2,1)}, u32[]{:S(2)}) %copy-start.2) | copy-done | bytes 524312
  3.3 0.0 copy-start.3
  3.3 0.7 %copy-done.3 = bf16[1,4,16,16]{3,2,1,0:T(8,128)(2,1)S(1)} copy-done((bf16[1,4,16,16]{3,2,1,0:T(8,128)(2,1)S(1)}, bf16[1,4,16,16]{3,2,1,0:T(8,128)(2,1)}, u32[]{:S(2)}) %copy-start.3) | copy-done | bytes 2072
  4.0 0.0 copy-start.4
  4.0 0.7 %copy-done.4 = s32[8]{0:T(128)S(1)} copy-done((s32[8]{0:T(128)S(1)}, s32[8]{0:T(128)}, u32[]{:S(2)}) %copy-start.4) | copy-done | bytes 56
  4.7 0.0 copy-start.5
  4.7 0.7 %copy-done.5 = s32[8]{0:T(128)S(1)} copy-done((s32[8]{0:T(128)S(1)}, s32[8]{0:T(128)}, u32[]{:S(2)}) %copy-start.5) | copy-done | bytes 56
  5.3 0.0 copy-start.6
  5.3 0.7 %copy-done.6 = s32[8]{0:T(128)S(1)} copy-done((s32[8]{0:T(128)S(1)}, s32[8]{0:T(128)}, u32[]{:S(2)}) %copy-start.6) | copy-done | bytes 56
  6.0 18.5 %shard_map.73 = (bf16[4,2,32,128]{3,2,1,0:T(8,128)(2,1)S(1)}, bf16[4,2,128,128]{3,2,1,0:T(8,128)(2,1)S(1)}, bf16[4,4,16,16]{3,2,1,0:T(8,128)(2,1)S(1)}) custom-call(s32[8]{0:T(128)S(1)} %copy-done.4, s32[8]{0:T(128)S(1)} %copy-done.5, s32[8]{0:T(128)S(1)} %copy-done.6, bf16[1,16,128,128]{3,2,1,0:T(8,128)(2,1)S(1)} %copy-done.1, ...), custom_call_target="tpu_custom_call" | custom-call | tf_op jit(solution)/shard_map/pallas_call | solution.py:193
  24.5 0.4 %fusion.7 = bf16[2,4,32,16,128]{4,2,3,1,0:T(8,128)(2,1)S(1)} fusion(bf16[2,128,16,128,1]{3,2,1,0,4:T(8,128)(2,1)S(1)} %bitcast.50, bf16[4,2,32,128]{3,2,1,0:T(8,128)(2,1)S(1)} %get-tuple-element.8), kind=kOutput, calls=%fused_computation.8 | convolution fusion | flops 134217728 | bytes 2162688 | tf_op jit(solution)/shard_map/wkml,klpr->kmwpr/dot_general | solution.py:273
  25.0 0.8 %fusion.3 = bf16[2,32,16,128]{3,2,1,0:T(8,128)(2,1)S(1)} fusion(bf16[2,4,32,16,128]{4,2,3,1,0:T(8,128)(2,1)S(1)} %fusion.7, bf16[4,2,128,128]{3,2,1,0:T(8,128)(2,1)S(1)} %get-tuple-element.10, bf16[4,4,16,16]{3,2,1,0:T(8,128)(2,1)S(1)} %get-tuple-element.9), kind=kOutput, calls=%fused_computation.5 | convolution fusion | flops 201981952 | bytes 1581056 | tf_op jit(solution)/shard_map/kmqvr,vktr->kmqt/dot_general | solution.py:275
  25.8 1.0 %copy.39 = bf16[1,2,512,128]{3,1,2,0:T(2,128)(2,1)} copy(bf16[1,2,512,128]{3,2,1,0:T(8,128)(2,1)S(1)} %bitcast.51) | data formatting | bytes 524288
Async XLA Ops:
  0.0 1.2 %copy-start = (bf16[2,128,16,128]{3,2,1,0:T(8,128)(2,1)S(1)}, bf16[2,128,16,128]{3,2,1,0:T(8,128)(2,1)}, u32[]{:S(2)}) copy-start(bf16[2,128,16,128]{3,2,1,0:T(8,128)(2,1)} %param.7) | copy-start | bytes 3145732
  1.2 1.0 %copy-start.1 = (bf16[1,16,128,128]{3,2,1,0:T(8,128)(2,1)S(1)}, bf16[1,16,128,128]{3,2,1,0:T(8,128)(2,1)}, u32[]{:S(2)}) copy-start(bf16[1,16,128,128]{3,2,1,0:T(8,128)(2,1)} %left_env_hbm.1) | copy-start | bytes 1572868
  2.3 1.0 %copy-start.2 = (bf16[1,16,128,128]{3,2,1,0:T(8,128)(2,1)S(1)}, bf16[1,16,128,128]{3,2,1,0:T(8,128)(2,1)}, u32[]{:S(2)}) copy-start(bf16[1,16,128,128]{3,2,1,0:T(8,128)(2,1)} %right_env_hbm.1) | copy-start | bytes 1572868
  3.3 0.7 %copy-start.3 = (bf16[1,4,16,16]{3,2,1,0:T(8,128)(2,1)S(1)}, bf16[1,4,16,16]{3,2,1,0:T(8,128)(2,1)}, u32[]{:S(2)}) copy-start(bf16[1,4,16,16]{3,2,1,0:T(8,128)(2,1)} %mpo.1) | copy-start | bytes 6148
  4.0 0.7 %copy-start.4 = (s32[8]{0:T(128)S(1)}, s32[8]{0:T(128)}, u32[]{:S(2)}) copy-start(s32[8]{0:T(128)} %left_local_hbm.1) | copy-start | bytes 100
  4.7 0.7 %copy-start.5 = (s32[8]{0:T(128)S(1)}, s32[8]{0:T(128)}, u32[]{:S(2)}) copy-start(s32[8]{0:T(128)} %right_owner_hbm.1) | copy-start | bytes 100
  5.3 0.7 %copy-start.6 = (s32[8]{0:T(128)S(1)}, s32[8]{0:T(128)}, u32[]{:S(2)}) copy-start(s32[8]{0:T(128)} %right_local_hbm.1) | copy-start | bytes 100

commit v4 on v3

--- a/solution.py
+++ b/solution.py
@@ -44,8 +44,17 @@
     *from_sector,
 ):
     blk_dev, local_rows = lenv.shape[1], lenv.shape[2]
+    piece = from_sector[0].shape[1]
+    cuts = to_sector.shape[2] // piece
+    chunks = blk_dev * cuts
     me = lax.axis_index("sector")
     z = lax.axis_index("mpo")
+    barrier = pltpu.get_barrier_semaphore()
+    for d in range(1, nsec):
+        pl.semaphore_signal(barrier, inc=1, device_id={"sector": lax.rem(me + d, nsec)}, device_id_type=MESH)
+    for d in range(1, nmpo):
+        pl.semaphore_signal(barrier, inc=1, device_id={"mpo": lax.rem(z + d, nmpo)}, device_id_type=MESH)
+
     loads = [
         pltpu.make_async_copy(src, dst, load_sem.at[i])
         for i, (src, dst) in enumerate(
@@ -61,12 +70,6 @@
     ]
     for load in loads:
         load.start()
-    barrier = pltpu.get_barrier_semaphore()
-    for d in range(1, nsec):
-        pl.semaphore_signal(barrier, inc=1, device_id={"sector": lax.rem(me + d, nsec)}, device_id_type=MESH)
-    for d in range(1, nmpo):
-        pl.semaphore_signal(barrier, inc=1, device_id={"mpo": lax.rem(z + d, nmpo)}, device_id_type=MESH)
-
     loads[0].wait()
     loads[1].wait()
     for k in range(blk_dev):
@@ -74,13 +77,16 @@
             to_sector[k, t] = right_env[right_local[t * blk_dev + k]]
     pl.semaphore_wait(barrier, nsec + nmpo - 2)
 
-    def sector_copy(k, d):
+    def span(c):
+        return pl.ds(c % cuts * piece, piece)
+
+    def sector_copy(c, d):
         peer = lax.rem(me + d, nsec)
         return pltpu.make_async_remote_copy(
-            src_ref=to_sector.at[k, peer],
-            dst_ref=from_sector[k].at[me],
-            send_sem=sector_send.at[k, d],
-            recv_sem=sector_recv.at[k, d],
+            src_ref=to_sector.at[c // cuts, peer, span(c)],
+            dst_ref=from_sector[c].at[me],
+            send_sem=sector_send.at[c, d],
+            recv_sem=sector_recv.at[c, d],
             device_id={"sector": peer},
             device_id_type=MESH,
         )
@@ -106,20 +112,20 @@
             device_id_type=MESH,
         )
 
-    def line_copy(origin, k, up):
+    def line_copy(origin, c, up):
         sems = up_send if up else down_send
         return pltpu.make_async_remote_copy(
-            src_ref=renv.at[origin, k],
-            dst_ref=renv.at[origin, k],
-            send_sem=sems.at[origin, k],
-            recv_sem=line_recv.at[origin, k],
+            src_ref=renv.at[origin, c // cuts, span(c)],
+            dst_ref=renv.at[origin, c // cuts, span(c)],
+            send_sem=sems.at[origin, c],
+            recv_sem=line_recv.at[origin, c],
             device_id={"mpo": z + 1 if up else z - 1},
             device_id_type=MESH,
         )
 
-    for k in range(blk_dev):
+    for c in range(chunks):
         for d in range(1, nsec):
-            sector_copy(k, d).start()
+            sector_copy(c, d).start()
     for d in range(1, nmpo):
         tensor_copy(d).start()
     loads[2].wait()
@@ -134,61 +140,63 @@
     loads[4].wait()
     loads[5].wait()
 
-    for k in range(blk_dev):
-        from_sector[k][me] = to_sector[k, me]
+    for c in range(chunks):
+        from_sector[c][me] = to_sector[c // cuts, me, span(c)]
         for d in range(1, nsec):
-            sector_copy(k, d).wait_recv()
-        renv[z, k] = from_sector[k][right_owner[me * blk_dev + k]]
+            sector_copy(c, d).wait_recv()
+        renv[z, c // cuts, span(c)] = from_sector[c][right_owner[me * blk_dev + c // cuts]]
 
         @pl.when(z < nmpo - 1)
         def _():
-            line_copy(z, k, True).start()
+            line_copy(z, c, True).start()
 
         @pl.when(z > 0)
         def _():
-            line_copy(z, k, False).start()
-
-    for d in range(1, nmpo):
-        for k in range(blk_dev):
+            line_copy(z, c, False).start()
+
+    for d in range(1, nmpo):
+        for c in range(chunks):
 
             @pl.when(z - d >= 0)
             def _():
-                line_copy(z - d, k, True).wait_recv()
+                line_copy(z - d, c, True).wait_recv()
 
                 @pl.when(z < nmpo - 1)
                 def _():
-                    line_copy(z - d, k, True).start()
+                    line_copy(z - d, c, True).start()
 
             @pl.when(z + d < nmpo)
             def _():
-                line_copy(z + d, k, False).wait_recv()
+                line_copy(z + d, c, False).wait_recv()
 
                 @pl.when(z > 0)
                 def _():
-                    line_copy(z + d, k, False).start()
+                    line_copy(z + d, c, False).start()
 
     for d in range(1, nmpo):
         left_copy(d).wait()
         tensor_copy(d).wait()
-    for k in range(blk_dev):
+    for c in range(chunks):
         for d in range(1, nsec):
-            sector_copy(k, d).wait_send()
+            sector_copy(c, d).wait_send()
         for d in range(nmpo):
 
             @pl.when((z < nmpo - 1) & (z - d >= 0))
             def _():
-                line_copy(z - d, k, True).wait_send()
+                line_copy(z - d, c, True).wait_send()
 
             @pl.when((z > 0) & (z + d < nmpo))
             def _():
-                line_copy(z + d, k, False).wait_send()
+                line_copy(z + d, c, False).wait_send()
 
 
 def gather(nsec, nmpo, mpo, left_env, right_env, left_local, right_owner, right_local, blk_dev):
     rows, width = right_env.shape[2:]
     local_rows = rows // nmpo
+    cuts = 2 if rows % 32 == 0 else 1
+    chunks = blk_dev * cuts
     vmem = pl.BlockSpec(memory_space=pltpu.VMEM)
-    hbm = pl.BlockSpec(memory_space=pl.ANY)
+    hbm = pl.BlockSpec(memory_space=pltpu.HBM)
     dma = pltpu.SemaphoreType.DMA
     return pl.pallas_call(
         functools.partial(exchange, nsec, nmpo),
@@ -208,19 +216,19 @@
             dma((6,)),
             pltpu.VMEM((blk_dev, nsec, rows, width), BF16),
             pltpu.VMEM((nmpo, blk_dev, local_rows, rows), BF16),
-            dma((blk_dev, nsec)),
-            dma((blk_dev, nsec)),
-            dma((nmpo,)),
-            dma((nmpo,)),
-            dma((nmpo,)),
-            dma((nmpo,)),
-            dma((nmpo, blk_dev)),
-            dma((nmpo, blk_dev)),
-            dma((nmpo, blk_dev)),
+            dma((chunks, nsec)),
+            dma((chunks, nsec)),
+            dma((nmpo,)),
+            dma((nmpo,)),
+            dma((nmpo,)),
+            dma((nmpo,)),
+            dma((nmpo, chunks)),
+            dma((nmpo, chunks)),
+            dma((nmpo, chunks)),
         ]
-        + [pltpu.VMEM((nsec, rows, width), BF16)] * blk_dev,
+        + [pltpu.VMEM((nsec, rows // cuts, width), BF16)] * chunks,
         compiler_params=pltpu.CompilerParams(
-            collective_id=0, has_side_effects=True, vmem_limit_bytes=40 * 2**20
+            collective_id=0, has_side_effects=True, vmem_limit_bytes=60 * 2**20
         ),
     )(left_local, right_owner, right_local, left_env, right_env, mpo)
 

time: 27.1 us -> 23.6 us (0.87)
  local copies, waits for them, and re-layouts: 6.96 us -> 2.21 us
  matrix products: 1.25 us -> 2.13 us
  Pallas kernels: 18.5 us -> 19 us
    unnamed x15 -> x7, local copies, waits for them, and re-layouts: 6.96 us -> 2.21 us
    dot_general x1, matrix products: 0.43 us -> 1.31 us  [body(): jnp.einsum('wkml,klpr->kmwpr', lenv, psi, preferred_element_type=F32)]
    pallas_call x1, Pallas kernels: 18.5 us -> 19 us  [gather(): pl.pallas_call(functools.partial(exchange, nsec, nmpo), out_shape=(jax.Sh...]
where the time goes in v4:
time: 23.6 us; the launch traced here: 23.4 us
  Pallas kernels  19 us (81%)
  local copies, waits for them, and re-layouts  2.21 us (9%)
  matrix products  2.13 us (9%)
    pallas_call x1, Pallas kernels, gather(): pl.pallas_call(functools.partial(exchange, nsec, nmpo), out_shape=(jax.Sh...  19 us
    unnamed x7, local copies, waits for them, and re-layouts  2.21 us
    dot_general x1, matrix products, body(): jnp.einsum('wkml,klpr->kmwpr', lenv, psi, preferred_element_type=F32)  1.31 us
    dot_general x1, matrix products, body(): jnp.einsum('kmqvr,vktr->kmqt', mixed, renv, preferred_element_type=F32)  0.82 us

profile of v4, /device:TPU:0, one launch (start us, length us, event | category | flops | bytes accessed | tf_op | source)
XLA Modules:
  0.0 23.4 jit_solution(12422091228021408804)
XLA Ops:
  0.0 0.0 copy-start
  0.0 1.2 %copy-done = bf16[2,128,16,128]{3,2,1,0:T(8,128)(2,1)S(1)} copy-done((bf16[2,128,16,128]{3,2,1,0:T(8,128)(2,1)S(1)}, bf16[2,128,16,128]{3,2,1,0:T(8,128)(2,1)}, u32[]{:S(2)}) %copy-start) | copy-done | bytes 1048600
  1.2 19.0 %shard_map.73 = (bf16[4,2,32,128]{3,2,1,0:T(8,128)(2,1)}, bf16[4,2,128,128]{3,2,1,0:T(8,128)(2,1)}, bf16[4,4,16,16]{3,2,1,0:T(8,128)(2,1)}) custom-call(s32[8]{0:T(128)} %left_local_hbm.1, s32[8]{0:T(128)} %right_owner_hbm.1, s32[8]{0:T(128)} %right_local_hbm.1, bf16[1,16,128,128]{3,2,1,0:T(8,128)(2,1)} %left_env_hbm.1, ...), custom_call_target="tpu_custom_call" | custom-call | tf_op jit(solution)/shard_map/pallas_call | solution.py:201
  20.3 0.0 copy-start.1
  20.3 0.0 copy-start.2
  20.3 1.3 %fusion.7 = bf16[2,4,32,16,128]{4,2,3,1,0:T(8,128)(2,1)S(1)} fusion(bf16[2,128,16,128,1]{3,2,1,0,4:T(8,128)(2,1)S(1)} %bitcast.50, bf16[4,2,32,128]{3,2,1,0:T(8,128)(2,1)} %get-tuple-element.8), kind=kOutput, calls=%fused_computation.8 | convolution fusion | flops 134217728 | bytes 2162688 | tf_op jit(solution)/shard_map/wkml,klpr->kmwpr/dot_general | solution.py:281
  21.6 0.0 copy-done.1
  21.6 0.0 copy-done.2
  21.6 0.8 %fusion.3 = bf16[2,32,16,128]{3,2,1,0:T(8,128)(2,1)S(1)} fusion(bf16[2,4,32,16,128]{4,2,3,1,0:T(8,128)(2,1)S(1)} %fusion.7, bf16[4,2,128,128]{3,2,1,0:T(8,128)(2,1)S(1)} %copy-done.1, bf16[4,4,16,16]{3,2,1,0:T(8,128)(2,1)S(1)} %copy-done.2), kind=kOutput, calls=%fused_computation.5 | convolution fusion | flops 201981952 | bytes 1581056 | tf_op jit(solution)/shard_map/kmqvr,vktr->kmqt/dot_general | solution.py:283
  22.5 1.0 %copy.39 = bf16[1,2,512,128]{3,1,2,0:T(2,128)(2,1)} copy(bf16[1,2,512,128]{3,2,1,0:T(8,128)(2,1)S(1)} %bitcast.51) | data formatting | bytes 524288
Async XLA Ops:
  0.0 1.2 %copy-start = (bf16[2,128,16,128]{3,2,1,0:T(8,128)(2,1)S(1)}, bf16[2,128,16,128]{3,2,1,0:T(8,128)(2,1)}, u32[]{:S(2)}) copy-start(bf16[2,128,16,128]{3,2,1,0:T(8,128)(2,1)} %param.7) | copy-start | bytes 3145732
  20.3 1.3 %copy-start.1 = (bf16[4,2,128,128]{3,2,1,0:T(8,128)(2,1)S(1)}, bf16[4,2,128,128]{3,2,1,0:T(8,128)(2,1)}, u32[]{:S(2)}) copy-start(bf16[4,2,128,128]{3,2,1,0:T(8,128)(2,1)} %get-tuple-element.10) | copy-start | bytes 786436
  20.3 1.3 %copy-start.2 = (bf16[4,4,16,16]{3,2,1,0:T(8,128)(2,1)S(1)}, bf16[4,4,16,16]{3,2,1,0:T(8,128)(2,1)}, u32[]{:S(2)}) copy-start(bf16[4,4,16,16]{3,2,1,0:T(8,128)(2,1)} %get-tuple-element.9) | copy-start | bytes 24580

commit v5 on v4

--- a/solution.py
+++ b/solution.py
@@ -72,9 +72,6 @@
         load.start()
     loads[0].wait()
     loads[1].wait()
-    for k in range(blk_dev):
-        for t in range(nsec):
-            to_sector[k, t] = right_env[right_local[t * blk_dev + k]]
     pl.semaphore_wait(barrier, nsec + nmpo - 2)
 
     def span(c):
@@ -123,9 +120,12 @@
             device_id_type=MESH,
         )
 
-    for c in range(chunks):
-        for d in range(1, nsec):
-            sector_copy(c, d).start()
+    for k in range(blk_dev):
+        for t in range(nsec):
+            to_sector[k, t] = right_env[right_local[t * blk_dev + k]]
+        for c in range(k * cuts, (k + 1) * cuts):
+            for d in range(1, nsec):
+                sector_copy(c, d).start()
     for d in range(1, nmpo):
         tensor_copy(d).start()
     loads[2].wait()
@@ -228,7 +228,7 @@
         ]
         + [pltpu.VMEM((nsec, rows // cuts, width), BF16)] * chunks,
         compiler_params=pltpu.CompilerParams(
-            collective_id=0, has_side_effects=True, vmem_limit_bytes=60 * 2**20
+            collective_id=0, has_side_effects=True, vmem_limit_bytes=63 * 2**20
         ),
     )(left_local, right_owner, right_local, left_env, right_env, mpo)
 

time: 23.6 us -> 22.8 us (0.966)
  local copies, waits for them, and re-layouts: 2.21 us -> 0.98 us
  matrix products: 2.13 us -> 2.55 us
    unnamed x7 -> x5, local copies, waits for them, and re-layouts: 2.21 us -> 0.98 us
    dot_general x1, matrix products: 1.31 us -> 1.74 us  [body(): jnp.einsum('wkml,klpr->kmwpr', lenv, psi, preferred_element_type=F32)]
where the time goes in v5:
time: 22.8 us; the launch traced here: 22.7 us
  Pallas kernels  19.1 us (84%)
  matrix products  2.55 us (11%)
  local copies, waits for them, and re-layouts  0.98 us (4%)
    pallas_call x1, Pallas kernels, gather(): pl.pallas_call(functools.partial(exchange, nsec, nmpo), out_shape=(jax.Sh...  19.1 us
    dot_general x1, matrix products, body(): jnp.einsum('wkml,klpr->kmwpr', lenv, psi, preferred_element_type=F32)  1.74 us
    unnamed x5, local copies, waits for them, and re-layouts  0.98 us
    dot_general x1, matrix products, body(): jnp.einsum('kmqvr,vktr->kmqt', mixed, renv, preferred_element_type=F32)  0.82 us

profile of v5, /device:TPU:0, one launch (start us, length us, event | category | flops | bytes accessed | tf_op | source)
XLA Modules:
  0.0 22.7 jit_solution(13580438047880194583)
XLA Ops:
  0.0 19.1 %shard_map.73 = (bf16[4,2,32,128]{3,2,1,0:T(8,128)(2,1)}, bf16[4,2,128,128]{3,2,1,0:T(8,128)(2,1)}, bf16[4,4,16,16]{3,2,1,0:T(8,128)(2,1)}) custom-call(s32[8]{0:T(128)} %left_local_hbm.1, s32[8]{0:T(128)} %right_owner_hbm.1, s32[8]{0:T(128)} %right_local_hbm.1, bf16[1,16,128,128]{3,2,1,0:T(8,128)(2,1)} %left_env_hbm.1, ...), custom_call_target="tpu_custom_call" | custom-call | tf_op jit(solution)/shard_map/pallas_call | solution.py:201
  19.1 0.0 copy-start
  19.1 0.0 copy-start.1
  19.1 1.7 %fusion.7 = bf16[2,4,32,16,128]{4,2,3,1,0:T(8,128)(2,1)S(1)} fusion(bf16[2,128,16,128,1]{3,2,1,0,4:T(8,128)(2,1)} %bitcast.50, bf16[4,2,32,128]{3,2,1,0:T(8,128)(2,1)} %get-tuple-element.8), kind=kOutput, calls=%fused_computation.8 | convolution fusion | flops 134217728 | bytes 2162688 | tf_op jit(solution)/shard_map/wkml,klpr->kmwpr/dot_general | solution.py:281
  20.8 0.0 copy-done
  20.8 0.0 copy-done.1
  20.9 0.8 %fusion.3 = bf16[2,32,16,128]{3,2,1,0:T(8,128)(2,1)S(1)} fusion(bf16[2,4,32,16,128]{4,2,3,1,0:T(8,128)(2,1)S(1)} %fusion.7, bf16[4,2,128,128]{3,2,1,0:T(8,128)(2,1)S(1)} %copy-done, bf16[4,4,16,16]{3,2,1,0:T(8,128)(2,1)S(1)} %copy-done.1), kind=kOutput, calls=%fused_computation.5 | convolution fusion | flops 201981952 | bytes 1581056 | tf_op jit(solution)/shard_map/kmqvr,vktr->kmqt/dot_general | solution.py:283
  21.7 1.0 %copy.39 = bf16[1,2,512,128]{3,1,2,0:T(2,128)(2,1)} copy(bf16[1,2,512,128]{3,2,1,0:T(8,128)(2,1)S(1)} %bitcast.51) | data formatting | bytes 524288
Async XLA Ops:
  19.1 1.8 %copy-start = (bf16[4,2,128,128]{3,2,1,0:T(8,128)(2,1)S(1)}, bf16[4,2,128,128]{3,2,1,0:T(8,128)(2,1)}, u32[]{:S(2)}) copy-start(bf16[4,2,128,128]{3,2,1,0:T(8,128)(2,1)} %get-tuple-element.10) | copy-start | bytes 786436
  19.1 1.8 %copy-start.1 = (bf16[4,4,16,16]{3,2,1,0:T(8,128)(2,1)S(1)}, bf16[4,4,16,16]{3,2,1,0:T(8,128)(2,1)}, u32[]{:S(2)}) copy-start(bf16[4,4,16,16]{3,2,1,0:T(8,128)(2,1)} %get-tuple-element.9) | copy-start | bytes 24580

commit v6 on v5

--- a/solution.py
+++ b/solution.py
@@ -38,9 +38,8 @@
     left_recv,
     tensor_send,
     tensor_recv,
-    up_send,
-    down_send,
-    line_recv,
+    own_send,
+    own_recv,
     *from_sector,
 ):
     blk_dev, local_rows = lenv.shape[1], lenv.shape[2]
@@ -109,14 +108,13 @@
             device_id_type=MESH,
         )
 
-    def line_copy(origin, c, up):
-        sems = up_send if up else down_send
-        return pltpu.make_async_remote_copy(
-            src_ref=renv.at[origin, c // cuts, span(c)],
-            dst_ref=renv.at[origin, c // cuts, span(c)],
-            send_sem=sems.at[origin, c],
-            recv_sem=line_recv.at[origin, c],
-            device_id={"mpo": z + 1 if up else z - 1},
+    def own_copy(c, d):
+        return pltpu.make_async_remote_copy(
+            src_ref=renv.at[z, c // cuts, span(c)],
+            dst_ref=renv.at[z, c // cuts, span(c)],
+            send_sem=own_send.at[d, c],
+            recv_sem=own_recv.at[d, c],
+            device_id={"mpo": lax.rem(z + d, nmpo)},
             device_id_type=MESH,
         )
 
@@ -146,48 +144,17 @@
             sector_copy(c, d).wait_recv()
         renv[z, c // cuts, span(c)] = from_sector[c][right_owner[me * blk_dev + c // cuts]]
 
-        @pl.when(z < nmpo - 1)
-        def _():
-            line_copy(z, c, True).start()
-
-        @pl.when(z > 0)
-        def _():
-            line_copy(z, c, False).start()
-
-    for d in range(1, nmpo):
-        for c in range(chunks):
-
-            @pl.when(z - d >= 0)
-            def _():
-                line_copy(z - d, c, True).wait_recv()
-
-                @pl.when(z < nmpo - 1)
-                def _():
-                    line_copy(z - d, c, True).start()
-
-            @pl.when(z + d < nmpo)
-            def _():
-                line_copy(z + d, c, False).wait_recv()
-
-                @pl.when(z > 0)
-                def _():
-                    line_copy(z + d, c, False).start()
+        for d in range(1, nmpo):
+            own_copy(c, d).start()
 
     for d in range(1, nmpo):
         left_copy(d).wait()
         tensor_copy(d).wait()
     for c in range(chunks):
+        for d in range(1, nmpo):
+            own_copy(c, d).wait()
         for d in range(1, nsec):
             sector_copy(c, d).wait_send()
-        for d in range(nmpo):
-
-            @pl.when((z < nmpo - 1) & (z - d >= 0))
-            def _():
-                line_copy(z - d, c, True).wait_send()
-
-            @pl.when((z > 0) & (z + d < nmpo))
-            def _():
-                line_copy(z + d, c, False).wait_send()
 
 
 def gather(nsec, nmpo, mpo, left_env, right_env, left_local, right_owner, right_local, blk_dev):
@@ -224,7 +191,6 @@
             dma((nmpo,)),
             dma((nmpo, chunks)),
             dma((nmpo, chunks)),
-            dma((nmpo, chunks)),
         ]
         + [pltpu.VMEM((nsec, rows // cuts, width), BF16)] * chunks,
         compiler_params=pltpu.CompilerParams(

time: 22.8 us -> 21 us (0.921)
  Pallas kernels: 19.1 us -> 17.2 us
    pallas_call x1, Pallas kernels: 19.1 us -> 17.2 us  [gather(): pl.pallas_call(functools.partial(exchange, nsec, nmpo), out_shape=(jax.Sh...]
where the time goes in v6:
time: 21 us; the launch traced here: 20.8 us
  Pallas kernels  17.2 us (82%)
  matrix products  2.55 us (12%)
  local copies, waits for them, and re-layouts  0.98 us (5%)
    pallas_call x1, Pallas kernels, gather(): pl.pallas_call(functools.partial(exchange, nsec, nmpo), out_shape=(jax.Sh...  17.2 us
    dot_general x1, matrix products, body(): jnp.einsum('wkml,klpr->kmwpr', lenv, psi, preferred_element_type=F32)  1.74 us
    unnamed x5, local copies, waits for them, and re-layouts  0.98 us
    dot_general x1, matrix products, body(): jnp.einsum('kmqvr,vktr->kmqt', mixed, renv, preferred_element_type=F32)  0.82 us

profile of v6, /device:TPU:0, one launch (start us, length us, event | category | flops | bytes accessed | tf_op | source)
XLA Modules:
  0.0 20.8 jit_solution(2597785784234187656)
XLA Ops:
  0.0 17.2 %shard_map.73 = (bf16[4,2,32,128]{3,2,1,0:T(8,128)(2,1)}, bf16[4,2,128,128]{3,2,1,0:T(8,128)(2,1)}, bf16[4,4,16,16]{3,2,1,0:T(8,128)(2,1)}) custom-call(s32[8]{0:T(128)} %left_local_hbm.1, s32[8]{0:T(128)} %right_owner_hbm.1, s32[8]{0:T(128)} %right_local_hbm.1, bf16[1,16,128,128]{3,2,1,0:T(8,128)(2,1)} %left_env_hbm.1, ...), custom_call_target="tpu_custom_call" | custom-call | tf_op jit(solution)/shard_map/pallas_call | solution.py:168
  17.2 0.0 copy-start
  17.2 0.0 copy-start.1
  17.3 1.7 %fusion.7 = bf16[2,4,32,16,128]{4,2,3,1,0:T(8,128)(2,1)S(1)} fusion(bf16[2,128,16,128,1]{3,2,1,0,4:T(8,128)(2,1)} %bitcast.50, bf16[4,2,32,128]{3,2,1,0:T(8,128)(2,1)} %get-tuple-element.8), kind=kOutput, calls=%fused_computation.8 | convolution fusion | flops 134217728 | bytes 2162688 | tf_op jit(solution)/shard_map/wkml,klpr->kmwpr/dot_general | solution.py:247
  19.0 0.0 copy-done
  19.0 0.0 copy-done.1
  19.0 0.8 %fusion.3 = bf16[2,32,16,128]{3,2,1,0:T(8,128)(2,1)S(1)} fusion(bf16[2,4,32,16,128]{4,2,3,1,0:T(8,128)(2,1)S(1)} %fusion.7, bf16[4,2,128,128]{3,2,1,0:T(8,128)(2,1)S(1)} %copy-done, bf16[4,4,16,16]{3,2,1,0:T(8,128)(2,1)S(1)} %copy-done.1), kind=kOutput, calls=%fused_computation.5 | convolution fusion | flops 201981952 | bytes 1581056 | tf_op jit(solution)/shard_map/kmqvr,vktr->kmqt/dot_general | solution.py:249
  19.8 1.0 %copy.39 = bf16[1,2,512,128]{3,1,2,0:T(2,128)(2,1)} copy(bf16[1,2,512,128]{3,2,1,0:T(8,128)(2,1)S(1)} %bitcast.51) | data formatting | bytes 524288
Async XLA Ops:
  17.2 1.8 %copy-start = (bf16[4,2,128,128]{3,2,1,0:T(8,128)(2,1)S(1)}, bf16[4,2,128,128]{3,2,1,0:T(8,128)(2,1)}, u32[]{:S(2)}) copy-start(bf16[4,2,128,128]{3,2,1,0:T(8,128)(2,1)} %get-tuple-element.10) | copy-start | bytes 786436
  17.2 1.8 %copy-start.1 = (bf16[4,4,16,16]{3,2,1,0:T(8,128)(2,1)S(1)}, bf16[4,4,16,16]{3,2,1,0:T(8,128)(2,1)}, u32[]{:S(2)}) copy-start(bf16[4,4,16,16]{3,2,1,0:T(8,128)(2,1)} %get-tuple-element.9) | copy-start | bytes 24580

commit v7 on v6

--- a/solution.py
+++ b/solution.py
@@ -40,6 +40,7 @@
     tensor_recv,
     own_send,
     own_recv,
+    far_send,
     *from_sector,
 ):
     blk_dev, local_rows = lenv.shape[1], lenv.shape[2]
@@ -115,6 +116,28 @@
             send_sem=own_send.at[d, c],
             recv_sem=own_recv.at[d, c],
             device_id={"mpo": lax.rem(z + d, nmpo)},
+            device_id_type=MESH,
+        )
+
+    relay = nmpo == 4
+    order = (2, 1, 3) if relay else tuple(range(1, nmpo))
+
+    def near(d):
+        if relay and d == 3:
+            return z > 0
+        if relay and d == 1:
+            return z < nmpo - 1
+        return z >= 0
+
+    def far_copy(c):
+        origin = lax.rem(z + 2, nmpo)
+        target = nmpo - 1 - origin
+        return pltpu.make_async_remote_copy(
+            src_ref=renv.at[origin, c // cuts, span(c)],
+            dst_ref=renv.at[origin, c // cuts, span(c)],
+            send_sem=far_send.at[c],
+            recv_sem=own_recv.at[lax.rem(target - origin + nmpo, nmpo), c],
+            device_id={"mpo": target},
             device_id_type=MESH,
         )
 
@@ -144,15 +167,38 @@
             sector_copy(c, d).wait_recv()
         renv[z, c // cuts, span(c)] = from_sector[c][right_owner[me * blk_dev + c // cuts]]
 
-        for d in range(1, nmpo):
-            own_copy(c, d).start()
+        for d in order:
+
+            @pl.when(near(d))
+            def _():
+                own_copy(c, d).start()
+
+    if relay:
+        for c in range(chunks):
+            own_copy(c, 2).wait_recv()
+
+            @pl.when((z > 0) & (z < nmpo - 1))
+            def _():
+                far_copy(c).start()
 
     for d in range(1, nmpo):
         left_copy(d).wait()
         tensor_copy(d).wait()
     for c in range(chunks):
-        for d in range(1, nmpo):
-            own_copy(c, d).wait()
+        for d in order:
+            if not (relay and d == 2):
+                own_copy(c, d).wait_recv()
+
+            @pl.when(near(d))
+            def _():
+                own_copy(c, d).wait_send()
+
+        if relay:
+
+            @pl.when((z > 0) & (z < nmpo - 1))
+            def _():
+                far_copy(c).wait_send()
+
         for d in range(1, nsec):
             sector_copy(c, d).wait_send()
 
@@ -191,6 +237,7 @@
             dma((nmpo,)),
             dma((nmpo, chunks)),
             dma((nmpo, chunks)),
+            dma((chunks,)),
         ]
         + [pltpu.VMEM((nsec, rows // cuts, width), BF16)] * chunks,
         compiler_params=pltpu.CompilerParams(

time: 21 us -> 21 us (level)
  no operation moved by 1% of the time
where the time goes in v7:
time: 21 us; the launch traced here: 20.9 us
  Pallas kernels  17.3 us (82%)
  matrix products  2.55 us (12%)
  local copies, waits for them, and re-layouts  0.98 us (5%)
    pallas_call x1, Pallas kernels, gather(): pl.pallas_call(functools.partial(exchange, nsec, nmpo), out_shape=(jax.Sh...  17.3 us
    dot_general x1, matrix products, body(): jnp.einsum('wkml,klpr->kmwpr', lenv, psi, preferred_element_type=F32)  1.73 us
    unnamed x5, local copies, waits for them, and re-layouts  0.98 us
    dot_general x1, matrix products, body(): jnp.einsum('kmqvr,vktr->kmqt', mixed, renv, preferred_element_type=F32)  0.82 us

profile of v7, /device:TPU:0, one launch (start us, length us, event | category | flops | bytes accessed | tf_op | source)
XLA Modules:
  0.0 20.9 jit_solution(15879792604321606543)
XLA Ops:
  0.0 17.3 %shard_map.73 = (bf16[4,2,32,128]{3,2,1,0:T(8,128)(2,1)}, bf16[4,2,128,128]{3,2,1,0:T(8,128)(2,1)}, bf16[4,4,16,16]{3,2,1,0:T(8,128)(2,1)}) custom-call(s32[8]{0:T(128)} %left_local_hbm.1, s32[8]{0:T(128)} %right_owner_hbm.1, s32[8]{0:T(128)} %right_local_hbm.1, bf16[1,16,128,128]{3,2,1,0:T(8,128)(2,1)} %left_env_hbm.1, ...), custom_call_target="tpu_custom_call" | custom-call | tf_op jit(solution)/shard_map/pallas_call | solution.py:214
  17.3 0.0 copy-start
  17.3 0.0 copy-start.1
  17.3 1.7 %fusion.7 = bf16[2,4,32,16,128]{4,2,3,1,0:T(8,128)(2,1)S(1)} fusion(bf16[2,128,16,128,1]{3,2,1,0,4:T(8,128)(2,1)} %bitcast.50, bf16[4,2,32,128]{3,2,1,0:T(8,128)(2,1)} %get-tuple-element.8), kind=kOutput, calls=%fused_computation.8 | convolution fusion | flops 134217728 | bytes 2162688 | tf_op jit(solution)/shard_map/wkml,klpr->kmwpr/dot_general | solution.py:294
  19.0 0.0 copy-done
  19.1 0.0 copy-done.1
  19.1 0.8 %fusion.3 = bf16[2,32,16,128]{3,2,1,0:T(8,128)(2,1)S(1)} fusion(bf16[2,4,32,16,128]{4,2,3,1,0:T(8,128)(2,1)S(1)} %fusion.7, bf16[4,2,128,128]{3,2,1,0:T(8,128)(2,1)S(1)} %copy-done, bf16[4,4,16,16]{3,2,1,0:T(8,128)(2,1)S(1)} %copy-done.1), kind=kOutput, calls=%fused_computation.5 | convolution fusion | flops 201981952 | bytes 1581056 | tf_op jit(solution)/shard_map/kmqvr,vktr->kmqt/dot_general | solution.py:296
  19.9 1.0 %copy.39 = bf16[1,2,512,128]{3,1,2,0:T(2,128)(2,1)} copy(bf16[1,2,512,128]{3,2,1,0:T(8,128)(2,1)S(1)} %bitcast.51) | data formatting | bytes 524288
Async XLA Ops:
  17.3 1.8 %copy-start = (bf16[4,2,128,128]{3,2,1,0:T(8,128)(2,1)S(1)}, bf16[4,2,128,128]{3,2,1,0:T(8,128)(2,1)}, u32[]{:S(2)}) copy-start(bf16[4,2,128,128]{3,2,1,0:T(8,128)(2,1)} %get-tuple-element.10) | copy-start | bytes 786436
  17.3 1.8 %copy-start.1 = (bf16[4,4,16,16]{3,2,1,0:T(8,128)(2,1)S(1)}, bf16[4,4,16,16]{3,2,1,0:T(8,128)(2,1)}, u32[]{:S(2)}) copy-start(bf16[4,4,16,16]{3,2,1,0:T(8,128)(2,1)} %get-tuple-element.9) | copy-start | bytes 24580

commit v8 on v6

--- a/solution.py
+++ b/solution.py
@@ -160,7 +160,7 @@
 def gather(nsec, nmpo, mpo, left_env, right_env, left_local, right_owner, right_local, blk_dev):
     rows, width = right_env.shape[2:]
     local_rows = rows // nmpo
-    cuts = 2 if rows % 32 == 0 else 1
+    cuts = 1
     chunks = blk_dev * cuts
     vmem = pl.BlockSpec(memory_space=pltpu.VMEM)
     hbm = pl.BlockSpec(memory_space=pltpu.HBM)

time: 21 us -> 20.7 us (0.986)
    pallas_call x1, Pallas kernels: 17.2 us -> 17 us  [gather(): pl.pallas_call(functools.partial(exchange, nsec, nmpo), out_shape=(jax.Sh...]
where the time goes in v8:
time: 20.7 us; the launch traced here: 20.6 us
  Pallas kernels  17 us (82%)
  matrix products  2.55 us (12%)
  local copies, waits for them, and re-layouts  0.98 us (5%)
    pallas_call x1, Pallas kernels, gather(): pl.pallas_call(functools.partial(exchange, nsec, nmpo), out_shape=(jax.Sh...  17 us
    dot_general x1, matrix products, body(): jnp.einsum('wkml,klpr->kmwpr', lenv, psi, preferred_element_type=F32)  1.73 us
    unnamed x5, local copies, waits for them, and re-layouts  0.98 us
    dot_general x1, matrix products, body(): jnp.einsum('kmqvr,vktr->kmqt', mixed, renv, preferred_element_type=F32)  0.82 us

profile of v8, /device:TPU:0, one launch (start us, length us, event | category | flops | bytes accessed | tf_op | source)
XLA Modules:
  0.0 20.6 jit_solution(14768623753089640123)
XLA Ops:
  0.0 17.0 %shard_map.73 = (bf16[4,2,32,128]{3,2,1,0:T(8,128)(2,1)}, bf16[4,2,128,128]{3,2,1,0:T(8,128)(2,1)}, bf16[4,4,16,16]{3,2,1,0:T(8,128)(2,1)}) custom-call(s32[8]{0:T(128)} %left_local_hbm.1, s32[8]{0:T(128)} %right_owner_hbm.1, s32[8]{0:T(128)} %right_local_hbm.1, bf16[1,16,128,128]{3,2,1,0:T(8,128)(2,1)} %left_env_hbm.1, ...), custom_call_target="tpu_custom_call" | custom-call | tf_op jit(solution)/shard_map/pallas_call | solution.py:168
  17.0 0.0 copy-start
  17.0 0.0 copy-start.1
  17.0 1.7 %fusion.7 = bf16[2,4,32,16,128]{4,2,3,1,0:T(8,128)(2,1)S(1)} fusion(bf16[2,128,16,128,1]{3,2,1,0,4:T(8,128)(2,1)} %bitcast.50, bf16[4,2,32,128]{3,2,1,0:T(8,128)(2,1)} %get-tuple-element.8), kind=kOutput, calls=%fused_computation.8 | convolution fusion | flops 134217728 | bytes 2162688 | tf_op jit(solution)/shard_map/wkml,klpr->kmwpr/dot_general | solution.py:247
  18.8 0.0 copy-done
  18.8 0.0 copy-done.1
  18.8 0.8 %fusion.3 = bf16[2,32,16,128]{3,2,1,0:T(8,128)(2,1)S(1)} fusion(bf16[2,4,32,16,128]{4,2,3,1,0:T(8,128)(2,1)S(1)} %fusion.7, bf16[4,2,128,128]{3,2,1,0:T(8,128)(2,1)S(1)} %copy-done, bf16[4,4,16,16]{3,2,1,0:T(8,128)(2,1)S(1)} %copy-done.1), kind=kOutput, calls=%fused_computation.5 | convolution fusion | flops 201981952 | bytes 1581056 | tf_op jit(solution)/shard_map/kmqvr,vktr->kmqt/dot_general | solution.py:249
  19.6 1.0 %copy.39 = bf16[1,2,512,128]{3,1,2,0:T(2,128)(2,1)} copy(bf16[1,2,512,128]{3,2,1,0:T(8,128)(2,1)S(1)} %bitcast.51) | data formatting | bytes 524288
Async XLA Ops:
  17.0 1.8 %copy-start = (bf16[4,2,128,128]{3,2,1,0:T(8,128)(2,1)S(1)}, bf16[4,2,128,128]{3,2,1,0:T(8,128)(2,1)}, u32[]{:S(2)}) copy-start(bf16[4,2,128,128]{3,2,1,0:T(8,128)(2,1)} %get-tuple-element.10) | copy-start | bytes 786436
  17.0 1.8 %copy-start.1 = (bf16[4,4,16,16]{3,2,1,0:T(8,128)(2,1)S(1)}, bf16[4,4,16,16]{3,2,1,0:T(8,128)(2,1)}, u32[]{:S(2)}) copy-start(bf16[4,4,16,16]{3,2,1,0:T(8,128)(2,1)} %get-tuple-element.9) | copy-start | bytes 24580

commit v9 on v8

--- a/solution.py
+++ b/solution.py
@@ -100,7 +100,7 @@
 
     def tensor_copy(d):
         return pltpu.make_async_remote_copy(
-            src_ref=mpo.at[0],
+            src_ref=tensor.at[z],
             dst_ref=tensor.at[z],
             send_sem=tensor_send.at[d],
             recv_sem=tensor_recv.at[d],
@@ -124,8 +124,6 @@
         for c in range(k * cuts, (k + 1) * cuts):
             for d in range(1, nsec):
                 sector_copy(c, d).start()
-    for d in range(1, nmpo):
-        tensor_copy(d).start()
     loads[2].wait()
     loads[3].wait()
     for k in range(blk_dev):
@@ -135,8 +133,10 @@
     for d in range(1, nmpo):
         left_copy(d).start()
     lenv[z] = to_mpo[z]
+    loads[5].wait()
+    for d in range(1, nmpo):
+        tensor_copy(d).start()
     loads[4].wait()
-    loads[5].wait()
 
     for c in range(chunks):
         from_sector[c][me] = to_sector[c // cuts, me, span(c)]

time: 20.7 us -> 20.7 us (level)
  no operation moved by 1% of the time
where the time goes in v9:
time: 20.7 us; the launch traced here: 20.6 us
  Pallas kernels  17 us (82%)
  matrix products  2.55 us (12%)
  local copies, waits for them, and re-layouts  0.98 us (5%)
    pallas_call x1, Pallas kernels, gather(): pl.pallas_call(functools.partial(exchange, nsec, nmpo), out_shape=(jax.Sh...  17 us
    dot_general x1, matrix products, body(): jnp.einsum('wkml,klpr->kmwpr', lenv, psi, preferred_element_type=F32)  1.73 us
    unnamed x5, local copies, waits for them, and re-layouts  0.98 us
    dot_general x1, matrix products, body(): jnp.einsum('kmqvr,vktr->kmqt', mixed, renv, preferred_element_type=F32)  0.82 us

profile of v9, /device:TPU:0, one launch (start us, length us, event | category | flops | bytes accessed | tf_op | source)
XLA Modules:
  0.0 20.6 jit_solution(8164072117360161065)
XLA Ops:
  0.0 17.0 %shard_map.73 = (bf16[4,2,32,128]{3,2,1,0:T(8,128)(2,1)}, bf16[4,2,128,128]{3,2,1,0:T(8,128)(2,1)}, bf16[4,4,16,16]{3,2,1,0:T(8,128)(2,1)}) custom-call(s32[8]{0:T(128)} %left_local_hbm.1, s32[8]{0:T(128)} %right_owner_hbm.1, s32[8]{0:T(128)} %right_local_hbm.1, bf16[1,16,128,128]{3,2,1,0:T(8,128)(2,1)} %left_env_hbm.1, ...), custom_call_target="tpu_custom_call" | custom-call | tf_op jit(solution)/shard_map/pallas_call | solution.py:168
  17.0 0.0 copy-start
  17.0 0.0 copy-start.1
  17.0 1.7 %fusion.7 = bf16[2,4,32,16,128]{4,2,3,1,0:T(8,128)(2,1)S(1)} fusion(bf16[2,128,16,128,1]{3,2,1,0,4:T(8,128)(2,1)} %bitcast.50, bf16[4,2,32,128]{3,2,1,0:T(8,128)(2,1)} %get-tuple-element.8), kind=kOutput, calls=%fused_computation.8 | convolution fusion | flops 134217728 | bytes 2162688 | tf_op jit(solution)/shard_map/wkml,klpr->kmwpr/dot_general | solution.py:247
  18.8 0.0 copy-done
  18.8 0.0 copy-done.1
  18.8 0.8 %fusion.3 = bf16[2,32,16,128]{3,2,1,0:T(8,128)(2,1)S(1)} fusion(bf16[2,4,32,16,128]{4,2,3,1,0:T(8,128)(2,1)S(1)} %fusion.7, bf16[4,2,128,128]{3,2,1,0:T(8,128)(2,1)S(1)} %copy-done, bf16[4,4,16,16]{3,2,1,0:T(8,128)(2,1)S(1)} %copy-done.1), kind=kOutput, calls=%fused_computation.5 | convolution fusion | flops 201981952 | bytes 1581056 | tf_op jit(solution)/shard_map/kmqvr,vktr->kmqt/dot_general | solution.py:249
  19.6 1.0 %copy.39 = bf16[1,2,512,128]{3,1,2,0:T(2,128)(2,1)} copy(bf16[1,2,512,128]{3,2,1,0:T(8,128)(2,1)S(1)} %bitcast.51) | data formatting | bytes 524288
Async XLA Ops:
  17.0 1.8 %copy-start = (bf16[4,2,128,128]{3,2,1,0:T(8,128)(2,1)S(1)}, bf16[4,2,128,128]{3,2,1,0:T(8,128)(2,1)}, u32[]{:S(2)}) copy-start(bf16[4,2,128,128]{3,2,1,0:T(8,128)(2,1)} %get-tuple-element.10) | copy-start | bytes 786436
  17.0 1.8 %copy-start.1 = (bf16[4,4,16,16]{3,2,1,0:T(8,128)(2,1)S(1)}, bf16[4,4,16,16]{3,2,1,0:T(8,128)(2,1)}, u32[]{:S(2)}) copy-start(bf16[4,4,16,16]{3,2,1,0:T(8,128)(2,1)} %get-tuple-element.9) | copy-start | bytes 24580
